TPU v7x, 128 devices: a whole 4x4x4 slice. The times are simulated.
128 devices in a mesh: bulk: 32 (over z, x_hi, y), grp: 4 (over x_lo, core).
Axes of the slice: x: 4 (x_hi: 2, x_lo: 2; x = x_hi * 2 + x_lo), y: 4, z: 4, core: 2. Of those that a mesh axis runs over, the one named last changes fastest.
Arguments:
- positions: float32 [3, 3145728], P(None, ('bulk', 'grp')), may hold values from -1 to 1
- normals: float32 [3, 3145728], P(None, ('bulk', 'grp')), may hold values from -6 to 6
- strength: float32 [3145728], P(('bulk', 'grp')), may hold values from -6 to 6
- near_index: int32 [24576, 6, 2], P(('bulk', 'grp')), may hold values from 0 to 191
- near_count: int32 [24576, 6], P(('bulk', 'grp')), may hold values from 0 to 2
Outputs:
- potential: float32 [3145728], P(('bulk', 'grp'))
Inputs may be any that keep to these rules, and one draw needn't show every extreme that they name: `near_index`: indexes a block among the 192 blocks of the round's partner device.
All inputs are finite; a program needn't handle non-finite values.
Results may differ from a plain program's by a relative error of at most 0.0003.
Values sent between devices are 32-bit elements; how exact they have to be, the bound alone decides.
No kernel may reach another device: no remote copies, remote signals or barrier semaphores. Data moves between devices by JAX's collectives and lax.ppermute only.
A program may use at most 64 MiB of HBM per device.

v0:
```python
import math

import jax
import jax.numpy as jnp
from jax import lax
from jax.sharding import PartitionSpec as P

DELTA2 = 0.05


def from_partner(x, axis, stride):
    return lax.ppermute(x, axis, [(i, i ^ 1 << stride) for i in range(lax.axis_size(axis))])


def tile_sum(targets, src_pos, src_nrm, src_q):
    high = lax.Precision.HIGHEST
    cross = targets[0][:, None, :, None] * src_pos[0][:, :, None, :]
    normal_dot = targets[0][:, None, :, None] * src_nrm[0][:, :, None, :]
    for comp in range(1, 3):
        cross = cross + targets[comp][:, None, :, None] * src_pos[comp][:, :, None, :]
        normal_dot = normal_dot + targets[comp][:, None, :, None] * src_nrm[comp][:, :, None, :]
    target_sq = jnp.sum(targets * targets, axis=0)
    source_sq = jnp.sum(src_pos * src_pos, axis=0)
    source_nd = jnp.sum(src_pos * src_nrm, axis=0)
    dist = target_sq[:, None, :, None] + source_sq[:, :, None, :] - 2.0 * cross + DELTA2
    kernel = (normal_dot - source_nd[:, :, None, :]) * lax.rsqrt(dist) / dist
    return jnp.einsum("tkij,tkj->tki", kernel, src_q, precision=high) * (1.0 / (4.0 * math.pi))


def near_terms(targets, src_pos, src_nrm, src_q, index_round, count_round):
    blocks = src_q.shape[0]
    slots = index_round.shape[1]
    pos_blocks = src_pos.reshape(3, blocks, -1)
    nrm_blocks = src_nrm.reshape(3, blocks, -1)
    chosen_pos = pos_blocks[:, index_round]
    chosen_nrm = nrm_blocks[:, index_round]
    chosen_q = src_q[index_round]
    slot_ids = jnp.arange(slots, dtype=jnp.int32)
    weight = (slot_ids[None, :] < count_round[:, None]).astype(jnp.float32)
    parts = tile_sum(targets, chosen_pos, chosen_nrm, chosen_q)
    return jnp.sum(parts * weight[:, :, None], axis=1)


def swap_grp(payload, bit):
    return from_partner((payload[0], payload[1], payload[2]), "grp", bit)


def shards(positions, normals, strength, near_index, near_count):
    blocks = near_index.shape[0]
    targets = positions.reshape(3, blocks, -1)
    own_n = normals.reshape(3, blocks, -1)
    own_q = strength.reshape(blocks, -1)
    total = tile_sum(targets, targets[:, :, None, :], own_n[:, :, None, :], own_q[:, None, :])[:, 0]
    top_bit = lax.axis_size("bulk").bit_length() - 2
    plan = [("grp", 0), ("grp", 1), ("bulk", 0), ("bulk", 1), ("bulk", 2), ("bulk", top_bit)]
    for step, (axis_name, bit) in enumerate(plan):
        index_round = near_index[:, step, :]
        count_round = near_count[:, step]
        if axis_name == "grp":
            far_pos, far_nrm, far_q = swap_grp((positions, normals, strength), bit)
            total = total + near_terms(
                targets, far_pos, far_nrm, far_q.reshape(blocks, -1), index_round, count_round
            )
        else:
            far_pos, far_nrm, far_q = from_partner((positions, normals, strength), "bulk", bit)
            total = total + near_terms(
                targets, far_pos, far_nrm, far_q.reshape(blocks, -1), index_round, count_round
            )
    return total.reshape(-1)


def solution(mesh):
    in_specs = (
        P(None, ("bulk", "grp")),
        P(None, ("bulk", "grp")),
        P(("bulk", "grp")),
        P(("bulk", "grp"), None, None),
        P(("bulk", "grp"), None),
    )
    out_specs = P(("bulk", "grp"))
    return jax.shard_map(shards, mesh=mesh, in_specs=in_specs, out_specs=out_specs, check_vma=False)
```

profile of v0, /device:TPU:0, one launch (start us, length us, event | category | flops | bytes accessed | tf_op | source)
XLA Modules:
  0.0 512.6 jit_solution(1694993429469336479)
XLA Ops:
  0.0 1.6 collective-permute-start.5
  1.7 1.6 collective-permute-start.8
  3.7 1.5 fusion.138
  5.3 1.6 multiply_reduce_fusion.13
  12.3 36.4 %fusion.90 = f32[192,1,128]{2,1,0:T(1,128)} fusion(f32[192,128,1]{1,2,0:T(1,128)S(1)} %bitcast.315, f32[192,128]{1,0:T(8,128)S(1)} %bitcast.283, f32[192,128]{1,0:T(8,128)S(1)} %bitcast.290, f32[192,128]{1,0:T(8,128)S(1)} %bitcast.276, f32[192,128]{1,0:T(8,128)S(1)} %bitcast.301, f32[192,128]{1,0:T(8,128)S(1)} %bitcast.308, f32[192,128]{1,0:T(8,128)S(1)} %bitcast.299, ...), kind=kOutput, calls=%fused_computation.115 | convolution fusion | flops 91226112 | bytes 983040 | tf_op jit(solution)/shard_map/tkij,tkj->tki/dot_general | solution.py:27
  48.8 3.0 collective-permute-start.11
  51.7 2.7 collective-permute-start.14
  54.5 3.9 collective-permute-start.17
  58.4 1.6 gather_fusion.2
  60.0 1.6 gather_fusion.5
  61.6 1.6 gather_fusion.8
  63.4 1.6 gather_fusion.11
  65.1 1.8 collective-permute-start.4
  66.9 1.6 gather_fusion.14
  68.6 1.6 gather_fusion.17
  70.2 1.9 collective-permute-start.7
  72.1 2.0 gather_fusion
  76.0 2.0 gather_fusion.1
  79.2 3.1 collective-permute-start.10
  82.3 2.3 gather_fusion.3
  84.6 1.3 fusion.127
  86.7 2.3 gather_fusion.4
  88.9 1.3 fusion.128
  90.2 2.7 collective-permute-start.13
  92.9 2.3 gather_fusion.6
  96.5 1.9 multiply_reduce_fusion.11
  98.4 2.3 gather_fusion.7
  100.7 1.3 fusion.130
  101.9 3.5 collective-permute-start.16
  105.5 2.3 gather_fusion.9
  109.0 1.9 multiply_reduce_fusion.9
  110.9 1.9 multiply_reduce_fusion.7
  112.8 2.2 gather_fusion.10
  115.1 2.3 gather_fusion.12
  118.6 3.1 gather_fusion.13
  123.0 1.9 multiply_reduce_fusion.5
  124.9 1.9 multiply_reduce_fusion.3
  126.8 2.3 gather_fusion.15
  130.4 2.3 gather_fusion.16
  132.7 1.3 fusion.135
  134.0 1.9 multiply_reduce_fusion.1
  135.9 1.3 fusion.136
  137.4 62.0 %fusion = f32[192,2,1,128]{3,2,1,0:T(1,128)S(1)} fusion(f32[192,2,128,1]{2,3,1,0:T(1,128)S(1)} %bitcast.239, f32[192,2,128]{2,1,0:T(2,128)S(1)} %bitcast.245, f32[192,2,128]{2,1,0:T(2,128)S(1)} %bitcast.244, f32[192,2,128]{2,1,0:T(2,128)S(1)} %bitcast.243, f32[192,2,128]{2,1,0:T(2,128)S(1)} %copy-done.53, f32[192,128]{1,0:T(8,128)S(1)} %bitcast.302, ...), kind=kOutput, calls=%fused_computation.24 | convolution fusion | flops 182452224 | bytes 2359296 | tf_op jit(solution)/shard_map/tkij,tkj->tki/dot_general | solution.py:27
  199.5 62.2 %fusion.1 = f32[192,2,1,128]{3,2,1,0:T(1,128)S(1)} fusion(f32[192,2,128,1]{2,3,1,0:T(1,128)S(1)} %bitcast.238, f32[192,2,128]{2,1,0:T(2,128)S(1)} %bitcast.254, f32[192,2,128]{2,1,0:T(2,128)S(1)} %bitcast.253, f32[192,2,128]{2,1,0:T(2,128)S(1)} %bitcast.252, f32[192,2,128]{2,1,0:T(2,128)S(1)} %copy-done.61, f32[192,2,128]{2,1,0:T(2,128)S(1)} %copy-done.60, ...), kind=kOutput, calls=%fused_computation.25 | convolution fusion | flops 182452224 | bytes 2359296 | tf_op jit(solution)/shard_map/tkij,tkj->tki/dot_general | solution.py:27
  262.8 62.0 %fusion.2 = f32[192,2,1,128]{3,2,1,0:T(1,128)S(1)} fusion(f32[192,2,128,1]{2,3,1,0:T(1,128)S(1)} %bitcast.237, f32[192,2,128]{2,1,0:T(2,128)S(1)} %bitcast.257, f32[192,2,128]{2,1,0:T(2,128)S(1)} %bitcast.256, f32[192,2,128]{2,1,0:T(2,128)S(1)} %bitcast.255, f32[192,2,128]{2,1,0:T(2,128)S(1)} %copy-done.55, f32[192,2,128]{2,1,0:T(2,128)S(1)} %copy-done.54, ...), kind=kOutput, calls=%fused_computation.26 | convolution fusion | flops 182452224 | bytes 2359296 | tf_op jit(solution)/shard_map/tkij,tkj->tki/dot_general | solution.py:27
  324.9 62.0 %fusion.3 = f32[192,2,1,128]{3,2,1,0:T(1,128)S(1)} fusion(f32[192,2,128,1]{2,3,1,0:T(1,128)S(1)} %bitcast.236, f32[192,2,128]{2,1,0:T(2,128)S(1)} %bitcast.266, f32[192,2,128]{2,1,0:T(2,128)S(1)} %bitcast.265, f32[192,2,128]{2,1,0:T(2,128)S(1)} %bitcast.264, f32[192,2,128]{2,1,0:T(2,128)S(1)} %copy-done.63, f32[192,2,128]{2,1,0:T(2,128)S(1)} %copy-done.62, ...), kind=kOutput, calls=%fused_computation.27 | convolution fusion | flops 182452224 | bytes 2359296 | tf_op jit(solution)/shard_map/tkij,tkj->tki/dot_general | solution.py:27
  387.2 62.0 %fusion.4 = f32[192,2,1,128]{3,2,1,0:T(1,128)S(1)} fusion(f32[192,2,128,1]{2,3,1,0:T(1,128)S(1)} %bitcast.235, f32[192,2,128]{2,1,0:T(2,128)S(1)} %bitcast.272, f32[192,2,128]{2,1,0:T(2,128)S(1)} %bitcast.271, f32[192,2,128]{2,1,0:T(2,128)S(1)} %bitcast.270, f32[192,2,128]{2,1,0:T(2,128)S(1)} %copy-done.57, f32[192,2,128]{2,1,0:T(2,128)S(1)} %copy-done.56, ...), kind=kOutput, calls=%fused_computation.28 | convolution fusion | flops 182452224 | bytes 2359296 | tf_op jit(solution)/shard_map/tkij,tkj->tki/dot_general | solution.py:27
  449.3 62.0 %fusion.5 = f32[192,2,1,128]{3,2,1,0:T(1,128)S(1)} fusion(f32[192,2,128,1]{2,3,1,0:T(1,128)S(1)} %bitcast.234, f32[192,2,128]{2,1,0:T(2,128)S(1)} %bitcast.275, f32[192,2,128]{2,1,0:T(2,128)S(1)} %bitcast.274, f32[192,2,128]{2,1,0:T(2,128)S(1)} %bitcast.273, f32[192,2,128]{2,1,0:T(2,128)S(1)} %copy-done.59, f32[192,2,128]{2,1,0:T(2,128)S(1)} %copy-done.58, ...), kind=kOutput, calls=%fused_computation.29 | convolution fusion | flops 182452224 | bytes 2359296 | tf_op jit(solution)/shard_map/tkij,tkj->tki/dot_general | solution.py:27
  (224 shorter events, 18.5 us)
Async XLA Ops:
  0.0 48.7 %collective-permute-start.2 = (f32[24576]{0:T(1024)}, f32[24576]{0:T(1024)S(1)}, u32[]{:S(2)}, u32[]{:S(2)}) collective-permute-start(f32[24576]{0:T(1024)} %param.7), channel_id=1, source_target_pairs={{0,1},{1,0},{2,3},{3,2},{4,5},{5,4},{6,7},{7,6},{8,9},{9,8},{10,11... | collective-permute-start | bytes 294920 | tf_op jit(solution)/shard_map/ppermute | solution.py:12
  0.0 51.7 %collective-permute-start.5 = (f32[24576]{0:T(1024)}, f32[24576]{0:T(1024)S(1)}, u32[]{:S(2)}, u32[]{:S(2)}) collective-permute-start(f32[24576]{0:T(1024)} %param.7), channel_id=1, source_target_pairs={{0,2},{1,3},{2,0},{3,1},{4,6},{5,7},{6,4},{7,5},{8,10},{9,11},{10,... | collective-permute-start | bytes 294920 | tf_op jit(solution)/shard_map/ppermute | solution.py:12
  1.7 52.8 %collective-permute-start.8 = (f32[24576]{0:T(1024)}, f32[24576]{0:T(1024)S(1)}, u32[]{:S(2)}, u32[]{:S(2)}) collective-permute-start(f32[24576]{0:T(1024)} %param.7), channel_id=1, source_target_pairs={{0,4},{4,0},{8,12},{12,8},{16,20},{20,16},{24,28},{28,24},{32,36},... | collective-permute-start | bytes 294920 | tf_op jit(solution)/shard_map/ppermute | solution.py:12
  3.2 67.0 %collective-permute-start = (f32[3,24576]{1,0:T(4,128)}, f32[3,24576]{1,0:T(4,128)S(1)}, u32[]{:S(2)}, u32[]{:S(2)}) collective-permute-start(f32[3,24576]{1,0:T(4,128)} %param.6), channel_id=1, source_target_pairs={{0,1},{1,0},{2,3},{3,2},{4,5},{5,4},{6,7},{7,6},{8,9},{9,8},{10,11... | collective-permute-start | bytes 884744 | tf_op jit(solution)/shard_map/ppermute | solution.py:12
  3.2 72.1 %collective-permute-start.1 = (f32[3,24576]{1,0:T(4,128)}, f32[3,24576]{1,0:T(4,128)S(1)}, u32[]{:S(2)}, u32[]{:S(2)}) collective-permute-start(f32[3,24576]{1,0:T(4,128)} %param.5), channel_id=1, source_target_pairs={{0,1},{1,0},{2,3},{3,2},{4,5},{5,4},{6,7},{7,6},{8,9},{9,8},{10,11... | collective-permute-start | bytes 884744 | tf_op jit(solution)/shard_map/ppermute | solution.py:12
  48.8 14.4 %collective-permute-start.11 = (f32[24576]{0:T(1024)S(1)}, f32[24576]{0:T(1024)S(1)}, u32[]{:S(2)}, u32[]{:S(2)}) collective-permute-start(f32[24576]{0:T(1024)S(1)} %copy-done.79), channel_id=1, source_target_pairs={{0,8},{4,12},{8,0},{12,4},{16,24},{20,28},{24,16},{28,20},{32,40},... | collective-permute-start | bytes 294920 | tf_op jit(solution)/shard_map/ppermute | solution.py:12
  51.7 13.3 %collective-permute-start.14 = (f32[24576]{0:T(1024)S(1)}, f32[24576]{0:T(1024)S(1)}, u32[]{:S(2)}, u32[]{:S(2)}) collective-permute-start(f32[24576]{0:T(1024)S(1)} %copy-done.79), channel_id=1, source_target_pairs={{0,16},{4,20},{8,24},{12,28},{16,0},{20,4},{24,8},{28,12},{32,48},... | collective-permute-start | bytes 294920 | tf_op jit(solution)/shard_map/ppermute | solution.py:12
  54.5 14.0 %collective-permute-start.17 = (f32[24576]{0:T(1024)S(1)}, f32[24576]{0:T(1024)S(1)}, u32[]{:S(2)}, u32[]{:S(2)}) collective-permute-start(f32[24576]{0:T(1024)S(1)} %copy-done.79), channel_id=1, source_target_pairs={{0,64},{4,68},{8,72},{12,76},{16,80},{20,84},{24,88},{28,92},{32,9... | collective-permute-start | bytes 294920 | tf_op jit(solution)/shard_map/ppermute | solution.py:12
  63.2 16.0 %collective-permute-start.3 = (f32[3,24576]{1,0:T(4,128)S(1)}, f32[3,24576]{1,0:T(4,128)}, u32[]{:S(2)}, u32[]{:S(2)}) collective-permute-start(f32[3,24576]{1,0:T(4,128)S(1)} %copy-done.8), channel_id=1, source_target_pairs={{0,2},{1,3},{2,0},{3,1},{4,6},{5,7},{6,4},{7,5},{8,10},{9,11},{10,... | collective-permute-start | bytes 884744 | tf_op jit(solution)/shard_map/ppermute | solution.py:12
  65.1 20.8 %collective-permute-start.4 = (f32[3,24576]{1,0:T(4,128)}, f32[3,24576]{1,0:T(4,128)}, u32[]{:S(2)}, u32[]{:S(2)}) collective-permute-start(f32[3,24576]{1,0:T(4,128)} %param.5), channel_id=1, source_target_pairs={{0,2},{1,3},{2,0},{3,1},{4,6},{5,7},{6,4},{7,5},{8,10},{9,11},{10,... | collective-permute-start | bytes 884744 | tf_op jit(solution)/shard_map/ppermute | solution.py:12
  68.5 21.7 %collective-permute-start.6 = (f32[3,24576]{1,0:T(4,128)S(1)}, f32[3,24576]{1,0:T(4,128)}, u32[]{:S(2)}, u32[]{:S(2)}) collective-permute-start(f32[3,24576]{1,0:T(4,128)S(1)} %copy-done.8), channel_id=1, source_target_pairs={{0,4},{4,0},{8,12},{12,8},{16,20},{20,16},{24,28},{28,24},{32,36},... | collective-permute-start | bytes 884744 | tf_op jit(solution)/shard_map/ppermute | solution.py:12
  70.2 28.1 %collective-permute-start.7 = (f32[3,24576]{1,0:T(4,128)}, f32[3,24576]{1,0:T(4,128)}, u32[]{:S(2)}, u32[]{:S(2)}) collective-permute-start(f32[3,24576]{1,0:T(4,128)} %param.5), channel_id=1, source_target_pairs={{0,4},{4,0},{8,12},{12,8},{16,20},{20,16},{24,28},{28,24},{32,36},... | collective-permute-start | bytes 884744 | tf_op jit(solution)/shard_map/ppermute | solution.py:12
  75.3 26.6 %collective-permute-start.9 = (f32[3,24576]{1,0:T(4,128)S(1)}, f32[3,24576]{1,0:T(4,128)}, u32[]{:S(2)}, u32[]{:S(2)}) collective-permute-start(f32[3,24576]{1,0:T(4,128)S(1)} %copy-done.8), channel_id=1, source_target_pairs={{0,8},{4,12},{8,0},{12,4},{16,24},{20,28},{24,16},{28,20},{32,40},... | collective-permute-start | bytes 884744 | tf_op jit(solution)/shard_map/ppermute | solution.py:12
  79.2 33.6 %collective-permute-start.10 = (f32[3,24576]{1,0:T(4,128)}, f32[3,24576]{1,0:T(4,128)S(1)}, u32[]{:S(2)}, u32[]{:S(2)}) collective-permute-start(f32[3,24576]{1,0:T(4,128)} %param.5), channel_id=1, source_target_pairs={{0,8},{4,12},{8,0},{12,4},{16,24},{20,28},{24,16},{28,20},{32,40},... | collective-permute-start | bytes 884744 | tf_op jit(solution)/shard_map/ppermute | solution.py:12
  85.9 29.2 %collective-permute-start.12 = (f32[3,24576]{1,0:T(4,128)S(1)}, f32[3,24576]{1,0:T(4,128)}, u32[]{:S(2)}, u32[]{:S(2)}) collective-permute-start(f32[3,24576]{1,0:T(4,128)S(1)} %copy-done.8), channel_id=1, source_target_pairs={{0,16},{4,20},{8,24},{12,28},{16,0},{20,4},{24,8},{28,12},{32,48},... | collective-permute-start | bytes 884744 | tf_op jit(solution)/shard_map/ppermute | solution.py:12
  90.2 28.4 %collective-permute-start.13 = (f32[3,24576]{1,0:T(4,128)}, f32[3,24576]{1,0:T(4,128)}, u32[]{:S(2)}, u32[]{:S(2)}) collective-permute-start(f32[3,24576]{1,0:T(4,128)} %param.5), channel_id=1, source_target_pairs={{0,16},{4,20},{8,24},{12,28},{16,0},{20,4},{24,8},{28,12},{32,48},... | collective-permute-start | bytes 884744 | tf_op jit(solution)/shard_map/ppermute | solution.py:12
  98.4 28.4 %collective-permute-start.15 = (f32[3,24576]{1,0:T(4,128)S(1)}, f32[3,24576]{1,0:T(4,128)}, u32[]{:S(2)}, u32[]{:S(2)}) collective-permute-start(f32[3,24576]{1,0:T(4,128)S(1)} %copy-done.8), channel_id=1, source_target_pairs={{0,64},{4,68},{8,72},{12,76},{16,80},{20,84},{24,88},{28,92},{32,9... | collective-permute-start | bytes 884744 | tf_op jit(solution)/shard_map/ppermute | solution.py:12
  101.9 28.5 %collective-permute-start.16 = (f32[3,24576]{1,0:T(4,128)}, f32[3,24576]{1,0:T(4,128)}, u32[]{:S(2)}, u32[]{:S(2)}) collective-permute-start(f32[3,24576]{1,0:T(4,128)} %param.5), channel_id=1, source_target_pairs={{0,64},{4,68},{8,72},{12,76},{16,80},{20,84},{24,88},{28,92},{32,9... | collective-permute-start | bytes 884744 | tf_op jit(solution)/shard_map/ppermute | solution.py:12
  137.3 62.0 %copy-start.28 = (f32[1,192,2,128]{3,0,2,1:T(1,128)S(1)}, f32[1,192,2,128]{3,0,2,1:T(1,128)}, u32[]{:S(2)}) copy-start(f32[1,192,2,128]{3,0,2,1:T(1,128)} %get-tuple-element.28) | copy-start | bytes 589828
  137.3 62.0 %copy-start.29 = (f32[1,192,2,128]{3,0,2,1:T(1,128)S(1)}, f32[1,192,2,128]{3,0,2,1:T(1,128)}, u32[]{:S(2)}) copy-start(f32[1,192,2,128]{3,0,2,1:T(1,128)} %get-tuple-element.29) | copy-start | bytes 589828
  137.4 62.0 %copy-start.30 = (f32[1,192,2,128]{3,0,2,1:T(1,128)S(1)}, f32[1,192,2,128]{3,0,2,1:T(1,128)}, u32[]{:S(2)}) copy-start(f32[1,192,2,128]{3,0,2,1:T(1,128)} %get-tuple-element.30) | copy-start | bytes 589828
  199.4 62.3 %copy-start.76 = (f32[192,2]{0,1:T(2,128)S(1)}, f32[192,2]{0,1:T(2,128)}, u32[]{:S(2)}) copy-start(f32[192,2]{0,1:T(2,128)} %compare_select_fusion.10) | copy-start | bytes 4612
  199.4 62.3 %copy-start.77 = (f32[192,2]{0,1:T(2,128)S(1)}, f32[192,2]{0,1:T(2,128)}, u32[]{:S(2)}) copy-start(f32[192,2]{0,1:T(2,128)} %compare_select_fusion.11) | copy-start | bytes 4612
  199.4 63.2 %copy-start.14 = (f32[384,128]{1,0:T(8,128)S(1)}, f32[384,128]{1,0:T(8,128)}, u32[]{:S(2)}) copy-start(f32[384,128]{1,0:T(8,128)} %gather_fusion.8) | copy-start | bytes 589828
  199.5 63.1 %copy-start.25 = (f32[1,192,2,128]{3,0,2,1:T(1,128)S(1)}, f32[1,192,2,128]{3,0,2,1:T(1,128)}, u32[]{:S(2)}) copy-start(f32[1,192,2,128]{3,0,2,1:T(1,128)} %get-tuple-element.31) | copy-start | bytes 589828
  199.5 63.1 %copy-start.26 = (f32[1,192,2,128]{3,0,2,1:T(1,128)S(1)}, f32[1,192,2,128]{3,0,2,1:T(1,128)}, u32[]{:S(2)}) copy-start(f32[1,192,2,128]{3,0,2,1:T(1,128)} %get-tuple-element.32) | copy-start | bytes 589828
  199.5 63.1 %copy-start.27 = (f32[1,192,2,128]{3,0,2,1:T(1,128)S(1)}, f32[1,192,2,128]{3,0,2,1:T(1,128)}, u32[]{:S(2)}) copy-start(f32[1,192,2,128]{3,0,2,1:T(1,128)} %get-tuple-element.33) | copy-start | bytes 589828
  199.5 63.1 %copy-start.31 = (f32[1,192,2,128]{3,0,2,1:T(1,128)S(1)}, f32[1,192,2,128]{3,0,2,1:T(1,128)}, u32[]{:S(2)}) copy-start(f32[1,192,2,128]{3,0,2,1:T(1,128)} %get-tuple-element.34) | copy-start | bytes 589828
  199.5 63.1 %copy-start.32 = (f32[1,192,2,128]{3,0,2,1:T(1,128)S(1)}, f32[1,192,2,128]{3,0,2,1:T(1,128)}, u32[]{:S(2)}) copy-start(f32[1,192,2,128]{3,0,2,1:T(1,128)} %get-tuple-element.35) | copy-start | bytes 589828
  199.5 63.1 %copy-start.33 = (f32[1,192,2,128]{3,0,2,1:T(1,128)S(1)}, f32[1,192,2,128]{3,0,2,1:T(1,128)}, u32[]{:S(2)}) copy-start(f32[1,192,2,128]{3,0,2,1:T(1,128)} %get-tuple-element.36) | copy-start | bytes 589828
  199.5 63.1 %copy-start.54 = (f32[192,2,128]{2,1,0:T(2,128)S(1)}, f32[192,2,128]{2,1,0:T(2,128)}, u32[]{:S(2)}) copy-start(f32[192,2,128]{2,1,0:T(2,128)} %get-tuple-element.9) | copy-start | bytes 589828
  199.5 63.1 %copy-start.55 = (f32[192,2,128]{2,1,0:T(2,128)S(1)}, f32[192,2,128]{2,1,0:T(2,128)}, u32[]{:S(2)}) copy-start(f32[192,2,128]{2,1,0:T(2,128)} %get-tuple-element.10) | copy-start | bytes 589828
  262.7 62.1 %copy-start.13 = (f32[384,128]{1,0:T(8,128)S(1)}, f32[384,128]{1,0:T(8,128)}, u32[]{:S(2)}) copy-start(f32[384,128]{1,0:T(8,128)} %gather_fusion.11) | copy-start | bytes 589828
  324.8 62.1 %copy-start.74 = (f32[192,2]{0,1:T(2,128)S(1)}, f32[192,2]{0,1:T(2,128)}, u32[]{:S(2)}) copy-start(f32[192,2]{0,1:T(2,128)} %compare_select_fusion.8) | copy-start | bytes 4612
  324.8 62.1 %copy-start.75 = (f32[192,2]{0,1:T(2,128)S(1)}, f32[192,2]{0,1:T(2,128)}, u32[]{:S(2)}) copy-start(f32[192,2]{0,1:T(2,128)} %compare_select_fusion.9) | copy-start | bytes 4612
  324.8 62.2 %copy-start.12 = (f32[384,128]{1,0:T(8,128)S(1)}, f32[384,128]{1,0:T(8,128)}, u32[]{:S(2)}) copy-start(f32[384,128]{1,0:T(8,128)} %gather_fusion.14) | copy-start | bytes 589828
  324.8 62.2 %copy-start.37 = (f32[1,192,2,128]{3,0,2,1:T(1,128)S(1)}, f32[1,192,2,128]{3,0,2,1:T(1,128)}, u32[]{:S(2)}) copy-start(f32[1,192,2,128]{3,0,2,1:T(1,128)} %get-tuple-element.43) | copy-start | bytes 589828
  324.8 62.2 %copy-start.38 = (f32[1,192,2,128]{3,0,2,1:T(1,128)S(1)}, f32[1,192,2,128]{3,0,2,1:T(1,128)}, u32[]{:S(2)}) copy-start(f32[1,192,2,128]{3,0,2,1:T(1,128)} %get-tuple-element.44) | copy-start | bytes 589828
  324.9 62.2 %copy-start.39 = (f32[1,192,2,128]{3,0,2,1:T(1,128)S(1)}, f32[1,192,2,128]{3,0,2,1:T(1,128)}, u32[]{:S(2)}) copy-start(f32[1,192,2,128]{3,0,2,1:T(1,128)} %get-tuple-element.45) | copy-start | bytes 589828
  324.9 62.2 %copy-start.46 = (f32[1,192,2,128]{3,0,2,1:T(1,128)S(1)}, f32[1,192,2,128]{3,0,2,1:T(1,128)}, u32[]{:S(2)}) copy-start(f32[1,192,2,128]{3,0,2,1:T(1,128)} %get-tuple-element.46) | copy-start | bytes 589828
  324.9 62.2 %copy-start.47 = (f32[1,192,2,128]{3,0,2,1:T(1,128)S(1)}, f32[1,192,2,128]{3,0,2,1:T(1,128)}, u32[]{:S(2)}) copy-start(f32[1,192,2,128]{3,0,2,1:T(1,128)} %get-tuple-element.47) | copy-start | bytes 589828
  324.9 62.2 %copy-start.48 = (f32[1,192,2,128]{3,0,2,1:T(1,128)S(1)}, f32[1,192,2,128]{3,0,2,1:T(1,128)}, u32[]{:S(2)}) copy-start(f32[1,192,2,128]{3,0,2,1:T(1,128)} %get-tuple-element.48) | copy-start | bytes 589828
  324.9 62.2 %copy-start.56 = (f32[192,2,128]{2,1,0:T(2,128)S(1)}, f32[192,2,128]{2,1,0:T(2,128)}, u32[]{:S(2)}) copy-start(f32[192,2,128]{2,1,0:T(2,128)} %get-tuple-element.13) | copy-start | bytes 589828
  324.9 62.2 %copy-start.57 = (f32[192,2,128]{2,1,0:T(2,128)S(1)}, f32[192,2,128]{2,1,0:T(2,128)}, u32[]{:S(2)}) copy-start(f32[192,2,128]{2,1,0:T(2,128)} %get-tuple-element.14) | copy-start | bytes 589828
  387.2 62.1 %copy-start.11 = (f32[384,128]{1,0:T(8,128)S(1)}, f32[384,128]{1,0:T(8,128)}, u32[]{:S(2)}) copy-start(f32[384,128]{1,0:T(8,128)} %gather_fusion.17) | copy-start | bytes 589828
  449.3 62.2 %copy-start.9 = (f32[192,128]{1,0:T(8,128)S(1)}, f32[192,128]{1,0:T(8,128)}, u32[]{:S(2)}) copy-start(f32[192,128]{1,0:T(8,128)} %get-tuple-element.77) | copy-start | bytes 294916
  449.3 62.2 %copy-start.10 = (f32[192,128]{1,0:T(8,128)S(1)}, f32[192,128]{1,0:T(8,128)}, u32[]{:S(2)}) copy-start(f32[192,128]{1,0:T(8,128)} %get-tuple-element.78) | copy-start | bytes 294916
  449.3 62.2 %copy-start.68 = (f32[192,1,128]{2,1,0:T(1,128)S(1)}, f32[192,1,128]{2,1,0:T(1,128)}, u32[]{:S(2)}) copy-start(f32[192,1,128]{2,1,0:T(1,128)} %fusion.90) | copy-start | bytes 294916
  (50 other events, 1571.6 us)
where the time goes:
time: 521 us; the launch traced here: 513 us
  matrix products  408 us (78%)
  local copies, waits for them, and re-layouts  56 us (11%)
  starting transfers between devices  28.1 us (5%)
  other arithmetic  18.4 us (4%)
    dot_general x7, matrix products, tile_sum(): jnp.einsum('tkij,tkj->tki', kernel, src_q, precision=high)  408 us
    ppermute x18, starting transfers between devices, from_partner(): lax.ppermute(x, axis, [(i, i ^ 1 << stride) for i in range(lax.axis_size(...  28.1 us
    gather x6, local copies, waits for them, and re-layouts, near_terms(): chosen_pos = pos_blocks[:, index_round]  14.1 us
    gather x6, local copies, waits for them, and re-layouts, near_terms(): chosen_nrm = nrm_blocks[:, index_round]  13.4 us
    reduce_sum x7, other arithmetic, tile_sum(): source_nd = jnp.sum(src_pos * src_nrm, axis=0)  13.1 us
  transfers between devices with their start and end apart: 18, of which 0 were waited for; matrix products, arithmetic and copies ran while one was open for 20% of the time, Pallas kernels for 0%

commit v1 on v0

v1 whole, which is shorter than its diff:
```python
import functools
import math

import jax
import jax.numpy as jnp
from jax import lax
from jax.experimental import pallas as pl
from jax.experimental.pallas import tpu as pltpu
from jax.sharding import PartitionSpec as P

DELTA2 = 0.05
BLK = 128
U = 32
KF = 32


def from_partner(x, axis, stride):
    return lax.ppermute(x, axis, [(i, i ^ 1 << stride) for i in range(lax.axis_size(axis))])


def split3(v):
    h = v.astype(jnp.bfloat16).astype(jnp.float32)
    r = v - h
    m = r.astype(jnp.bfloat16).astype(jnp.float32)
    return h, m, r - m


def row(ref, c, b):
    return jnp.broadcast_to(ref[c, pl.ds(b, 1), :], (8, BLK))


def by_row(sub, a, b, c, d):
    k = sub & 3
    return jnp.where(k == 0, a, jnp.where(k == 1, b, jnp.where(k == 2, c, d)))


def target_features(msg, b, sub):
    x, y, z = row(msg, 0, b), row(msg, 1, b), row(msg, 2, b)
    h, m, l = split3(by_row(sub, x, y, z, x * x + y * y + z * z + DELTA2))
    last, low = (sub & 3) == 3, sub < 4
    h1 = jnp.where(last, 1.0, h)
    bands = [h1, jnp.where(low, h1, jnp.where(last, h, m)), jnp.where(low, m, l), jnp.zeros_like(h)]
    return jnp.concatenate(bands, axis=0)


def source_bands(v, sub, unit):
    h, m, l = split3(v)
    last, low = (sub & 3) == 3, sub < 4
    hu = jnp.where(last, unit, h)
    mu = jnp.where(last, unit, m)
    bands = [jnp.where(low, h, m), jnp.where(low, l, hu), jnp.where(low, mu, hu), jnp.zeros_like(h)]
    return jnp.concatenate(bands, axis=0).astype(jnp.bfloat16)


def source_features(msg, b, sub):
    x, y, z = row(msg, 0, b), row(msg, 1, b), row(msg, 2, b)
    u, v, w = row(msg, 3, b), row(msg, 4, b), row(msg, 5, b)
    dist = by_row(sub, -2.0 * x, -2.0 * y, -2.0 * z, x * x + y * y + z * z)
    num = by_row(sub, u, v, w, -(x * u + y * v + z * w))
    return source_bands(dist, sub, 1.0), source_bands(num, sub, 0.0)


def phase_kernel(nb, rounds, own, last, index, count, *refs):
    n_src = len(rounds) + (1 if own else 0)
    mine = refs[0]
    msgs = refs[:1] if own else ()
    msgs = tuple(msgs) + tuple(refs[1:1 + len(rounds)])
    rest = refs[1 + len(rounds):]
    if not own:
        before, rest = rest[0], rest[1:]
    out, left, right, acc, work = rest

    sub = lax.broadcasted_iota(jnp.int32, (8, BLK), 0)
    lane = lax.broadcasted_iota(jnp.int32, (8, BLK), 1)
    group = lane >> 3

    if own:
        acc[...] = jnp.zeros_like(acc)
    else:
        acc[pl.ds(0, nb)] = before[...]
    left[pl.ds(nb * BLK, BLK), :] = jnp.zeros((BLK, BLK), jnp.bfloat16)

    def build_left(b, _):
        f = target_features(mine, b, sub)
        left[pl.ds(pl.multiple_of(b * BLK, BLK), BLK), :KF] = f.T.astype(jnp.bfloat16)
        return 0

    lax.fori_loop(0, nb, build_left, 0, unroll=4)

    n = jnp.int32(0)
    for k, msg in enumerate(msgs):
        r = -1 if own and k == 0 else rounds[k - (1 if own else 0)]

        def build_right(b, n, msg=msg, k=k, r=r):
            d, f = source_features(msg, b, sub)
            right[k * nb + b, :, :BLK] = d
            right[k * nb + b, :, BLK:] = f
            if r < 0:
                work[n] = (b << 12) + b
                return n + 1
            c = count[r * nb + b]
            base = (b << 12) + k * nb
            work[n] = base + index[(2 * r) * nb + b]
            work[n + 1] = base + index[(2 * r + 1) * nb + b]
            return n + c

        n = lax.fori_loop(0, nb, build_right, n, unroll=4)

    for u in range(U):
        work[n + u] = jnp.int32(nb << 12)

    def tiles(i, _):
        codes = [work[i * U + u] for u in range(U)]
        prods = []
        for code in codes:
            a = left[pl.ds(pl.multiple_of((code >> 12) * BLK, BLK), BLK), :KF]
            prods.append(jnp.dot(a, right[code & 4095], preferred_element_type=jnp.float32))
        for code, p in zip(codes, prods):
            s = lax.rsqrt(p[:, :BLK])
            w = p[:, BLK:] * (s * (s * s))
            total = jnp.broadcast_to(jnp.sum(w, axis=1, keepdims=True), (BLK, BLK)).reshape(16, 8, BLK)
            a = total[0]
            for g in range(1, 16):
                a = jnp.where(group == g, total[g], a)
            acc[code >> 12] += a
        return 0

    lax.fori_loop(0, (n + U - 1) // U, tiles, 0)

    if last:
        keep = (lane & 7) == sub

        def finish(i, _):
            a = acc[pl.ds(i * 8, 8)]
            out[pl.ds(pl.multiple_of(i * 8, 8), 8), :] = jnp.sum(jnp.where(keep[None], a, 0.0), axis=1)
            return 0

        lax.fori_loop(0, nb // 8, finish, 0)
    else:
        out[...] = acc[pl.ds(0, nb)]


def phase(name, rounds, own, last, index, count, mine, msgs, before):
    nb = mine.shape[1]
    n_src = len(rounds) + (1 if own else 0)
    smem, vmem = pl.BlockSpec(memory_space=pltpu.SMEM), pl.BlockSpec(memory_space=pltpu.VMEM)
    args = [index, count, mine, *msgs] + ([] if own else [before])
    shape = (nb, BLK) if last else (nb, 8, BLK)
    return pl.pallas_call(
        functools.partial(phase_kernel, nb, tuple(rounds), own, last),
        out_shape=jax.ShapeDtypeStruct(shape, jnp.float32),
        in_specs=[smem, smem] + [vmem] * (len(args) - 2),
        out_specs=vmem,
        scratch_shapes=[
            pltpu.VMEM(((nb + 1) * BLK, BLK), jnp.bfloat16),
            pltpu.VMEM((n_src * nb, KF, 2 * BLK), jnp.bfloat16),
            pltpu.VMEM((nb + 1, 8, BLK), jnp.float32),
            pltpu.SMEM((n_src * 2 * nb + 2 * U,), jnp.int32),
        ],
        compiler_params=pltpu.CompilerParams(vmem_limit_bytes=40 << 20),
        cost_estimate=pl.CostEstimate(flops=n_src * 2_000_000_000, bytes_accessed=n_src * 1_000_000, transcendentals=0),
        name=name,
    )(*args)


def shards(positions, normals, strength, near_index, near_count):
    nb = near_index.shape[0]
    scaled = normals * (strength * (1.0 / (4.0 * math.pi)))[None]
    mine = jnp.concatenate([positions, scaled], axis=0).reshape(6, nb, BLK)
    top_bit = lax.axis_size("bulk").bit_length() - 2
    plan = [("grp", 0), ("grp", 1), ("bulk", 0), ("bulk", 1), ("bulk", 2), ("bulk", top_bit)]
    far = [from_partner(mine, axis, bit) for axis, bit in plan]
    index = near_index.transpose(1, 2, 0).reshape(-1)
    count = near_count.T.reshape(-1)
    a = phase("own_core", [0], True, False, index, count, mine, [far[0]], None)
    b = phase("mid", [5, 1, 2], False, False, index, count, mine, [far[5], far[1], far[2]], a)
    c = phase("end", [3, 4], False, True, index, count, mine, [far[3], far[4]], b)
    return c.reshape(-1)


def solution(mesh):
    in_specs = (
        P(None, ("bulk", "grp")),
        P(None, ("bulk", "grp")),
        P(("bulk", "grp")),
        P(("bulk", "grp"), None, None),
        P(("bulk", "grp"), None),
    )
    out_specs = P(("bulk", "grp"))
    return jax.shard_map(shards, mesh=mesh, in_specs=in_specs, out_specs=out_specs, check_vma=False)
```

time: 521 us -> 83.2 us (0.16)
  the two profiles are of different devices: /device:TPU:0 before, /device:TPU:2 now
where the time goes in v1:
time: 83.2 us; the launch traced here: 81.9 us
  Pallas kernels  67.8 us (81%)
  starting transfers between devices  11.5 us (14%)
  other arithmetic  2.21 us (3%)
    pallas_call x3, Pallas kernels, phase(): pl.pallas_call(functools.partial(phase_kernel, nb, tuple(rounds), own, la...  67.8 us
    ppermute x6, starting transfers between devices, from_partner(): lax.ppermute(x, axis, [(i, i ^ 1 << stride) for i in range(lax.axis_size(...  11.5 us
    mul x2, other arithmetic, shards(): scaled = normals * (strength * (1.0 / (4.0 * math.pi)))[None]  2.05 us
  transfers between devices with their start and end apart: 6, of which 0 were waited for; matrix products, arithmetic and copies ran while one was open for 0% of the time, Pallas kernels for 57%

profile of v1, /device:TPU:2, one launch (start us, length us, event | category | flops | bytes accessed | tf_op | source)
XLA Modules:
  0.0 81.9 jit_solution(13848824723046420543)
XLA Ops:
  0.0 0.9 %broadcast_multiply_fusion.1 = f32[24576]{0:T(1024)S(1)} fusion(f32[24576]{0:T(1024)} %param.7), kind=kLoop, calls=%fused_computation.3 | loop fusion | flops 24576 | bytes 196608 | tf_op jit(solution)/shard_map/mul | solution.py:168
  0.9 0.0 copy-start
  0.9 1.1 %broadcast_multiply_fusion = f32[3,24576]{1,0:T(4,128)S(1)} fusion(f32[3,24576]{1,0:T(4,128)} %param.6, f32[24576]{0:T(1024)S(1)} %broadcast_multiply_fusion.1), kind=kLoop, calls=%fused_computation.2 | loop fusion | flops 73728 | bytes 688128 | tf_op jit(solution)/shard_map/mul | solution.py:168
  2.1 0.0 copy-done
  2.1 0.2 maximum_bitcast_fusion
  2.2 0.0 copy-start.2
  2.3 0.1 copy.8
  2.4 0.0 copy-start.1
  2.4 0.1 collective-permute-start.5
  2.5 1.7 %collective-permute-start.4 = (f32[6,192,128]{2,1,0:T(8,128)S(1)}, f32[6,192,128]{2,1,0:T(8,128)S(1)}, u32[]{:S(2)}, u32[]{:S(2)}) collective-permute-start(f32[6,192,128]{2,1,0:T(8,128)S(1)} %bitcast.9), channel_id=1, source_target_pairs={{0,4},{4,0},{8,12},{12,8},{16,20},{20,16},{24,28},{28,24},{32,36},... | collective-permute-start | bytes 1769480 | tf_op jit(solution)/shard_map/ppermute | solution.py:18
  4.1 0.5 collective-permute-start.3
  4.7 3.9 %collective-permute-start.2 = (f32[6,192,128]{2,1,0:T(8,128)S(1)}, f32[6,192,128]{2,1,0:T(8,128)S(1)}, u32[]{:S(2)}, u32[]{:S(2)}) collective-permute-start(f32[6,192,128]{2,1,0:T(8,128)S(1)} %bitcast.11), channel_id=1, source_target_pairs={{0,64},{4,68},{8,72},{12,76},{16,80},{20,84},{24,88},{28,92},{32,9... | collective-permute-start | bytes 1769480 | tf_op jit(solution)/shard_map/ppermute | solution.py:18
  8.6 2.4 %collective-permute-start.1 = (f32[6,192,128]{2,1,0:T(8,128)S(1)}, f32[6,192,128]{2,1,0:T(8,128)S(1)}, u32[]{:S(2)}, u32[]{:S(2)}) collective-permute-start(f32[6,192,128]{2,1,0:T(8,128)S(1)} %bitcast.12), channel_id=1, source_target_pairs={{0,16},{4,20},{8,24},{12,28},{16,0},{20,4},{24,8},{28,12},{32,48},... | collective-permute-start | bytes 1769480 | tf_op jit(solution)/shard_map/ppermute | solution.py:18
  11.0 0.0 copy-done.2
  11.0 0.1 reshape.14.count
  11.1 0.0 copy-done.1
  11.1 0.1 reshape.13.index
  11.1 0.0 collective-permute-done.5.refs_1_
  11.1 2.9 %collective-permute-start = (f32[6,192,128]{2,1,0:T(8,128)S(1)}, f32[6,192,128]{2,1,0:T(8,128)S(1)}, u32[]{:S(2)}, u32[]{:S(2)}) collective-permute-start(f32[6,192,128]{2,1,0:T(8,128)S(1)} %bitcast.13), channel_id=1, source_target_pairs={{0,8},{4,12},{8,0},{12,4},{16,24},{20,28},{24,16},{28,20},{32,40},... | collective-permute-start | bytes 1769480 | tf_op jit(solution)/shard_map/ppermute | solution.py:18
  14.1 20.6 %own_core.1.refs_4_ = f32[192,8,128]{2,1,0:T(8,128)S(1)} custom-call(s32[2304]{0:T(1024)S(1)} %reshape.13.index, s32[1152]{0:T(1024)S(1)} %reshape.14.count, f32[6,192,128]{2,1,0:T(8,128)S(1)} %bitcast.14, f32[6,192,128]{2,1,0:T(8,128)} %collective-permute-done.5.refs_1_), custom_call_target="tpu_custom_call" | custom-call | flops 4000000000 | bytes 2000000 | tf_op jit(solution)/shard_map/own_core/pallas_call | solution.py:149
  34.7 0.0 collective-permute-done.4.refs_3_
  34.7 0.0 collective-permute-done.3.refs_2_
  34.7 0.0 collective-permute-done.2.refs_1_
  34.7 25.9 %mid.1.refs_3_ = f32[192,8,128]{2,1,0:T(8,128)S(1)} custom-call(s32[2304]{0:T(1024)S(1)} %reshape.13.index, s32[1152]{0:T(1024)S(1)} %reshape.14.count, f32[6,192,128]{2,1,0:T(8,128)S(1)} %bitcast.15, f32[6,192,128]{2,1,0:T(8,128)S(1)} %collective-permute-done.2.refs_1_, f32[6,192,128]{2,1,0:T(8,128)S(1)} %collective-permute-done.3.refs_2_, ...), custom_call_target="tpu_custom_call" | custom-call | flops 6000000000 | bytes 3000000 | tf_op jit(solution)/shard_map/mid/pallas_call | solution.py:149
  60.6 0.0 collective-permute-done.1.refs_2_
  60.6 0.0 collective-permute-done.refs_1_
  60.6 21.3 %end.1 = f32[192,128]{1,0:T(8,128)} custom-call(s32[2304]{0:T(1024)S(1)} %reshape.13.index, s32[1152]{0:T(1024)S(1)} %reshape.14.count, f32[6,192,128]{2,1,0:T(8,128)S(1)} %bitcast.16, f32[6,192,128]{2,1,0:T(8,128)S(1)} %collective-permute-done.refs_1_, f32[6,192,128]{2,1,0:T(8,128)S(1)} %collective-permute-done.1.refs_2_, f32[192,8,128]{2,1,0:T(8,128)S(1)} %mid.1.refs_3_), custom_call_target="tpu_custom_call" | custom-call | flops 4000000000 | bytes 2000000 | tf_op jit(solution)/shard_map/end/pallas_call | solution.py:149
Async XLA Ops:
  0.9 1.2 %copy-start = (f32[3,24576]{1,0:T(4,128)S(1)}, f32[3,24576]{1,0:T(4,128)}, u32[]{:S(2)}) copy-start(f32[3,24576]{1,0:T(4,128)} %param.5) | copy-start | bytes 884740
  2.2 8.7 %copy-start.2 = (s32[192,6]{0,1:T(8,128)S(1)}, s32[192,6]{0,1:T(8,128)}, u32[]{:S(2)}) copy-start(s32[192,6]{0,1:T(8,128)} %param.9) | copy-start | bytes 13828
  2.4 8.7 %copy-start.1 = (s32[192,6,2]{0,2,1:T(2,128)S(1)}, s32[192,6,2]{0,2,1:T(2,128)}, u32[]{:S(2)}) copy-start(s32[192,6,2]{0,2,1:T(2,128)} %param.8) | copy-start | bytes 27652
  2.4 8.7 %collective-permute-start.5 = (f32[6,192,128]{2,1,0:T(8,128)S(1)}, f32[6,192,128]{2,1,0:T(8,128)}, u32[]{:S(2)}, u32[]{:S(2)}) collective-permute-start(f32[6,192,128]{2,1,0:T(8,128)S(1)} %bitcast.8), channel_id=1, source_target_pairs={{0,1},{1,0},{2,3},{3,2},{4,5},{5,4},{6,7},{7,6},{8,9},{9,8},{10,11... | collective-permute-start | bytes 1769480 | tf_op jit(solution)/shard_map/ppermute | solution.py:18
  2.5 32.2 %collective-permute-start.4 = (f32[6,192,128]{2,1,0:T(8,128)S(1)}, f32[6,192,128]{2,1,0:T(8,128)S(1)}, u32[]{:S(2)}, u32[]{:S(2)}) collective-permute-start(f32[6,192,128]{2,1,0:T(8,128)S(1)} %bitcast.9), channel_id=1, source_target_pairs={{0,4},{4,0},{8,12},{12,8},{16,20},{20,16},{24,28},{28,24},{32,36},... | collective-permute-start | bytes 1769480 | tf_op jit(solution)/shard_map/ppermute | solution.py:18
  4.1 30.5 %collective-permute-start.3 = (f32[6,192,128]{2,1,0:T(8,128)S(1)}, f32[6,192,128]{2,1,0:T(8,128)S(1)}, u32[]{:S(2)}, u32[]{:S(2)}) collective-permute-start(f32[6,192,128]{2,1,0:T(8,128)S(1)} %bitcast.10), channel_id=1, source_target_pairs={{0,2},{1,3},{2,0},{3,1},{4,6},{5,7},{6,4},{7,5},{8,10},{9,11},{10,... | collective-permute-start | bytes 1769480 | tf_op jit(solution)/shard_map/ppermute | solution.py:18
  4.7 30.0 %collective-permute-start.2 = (f32[6,192,128]{2,1,0:T(8,128)S(1)}, f32[6,192,128]{2,1,0:T(8,128)S(1)}, u32[]{:S(2)}, u32[]{:S(2)}) collective-permute-start(f32[6,192,128]{2,1,0:T(8,128)S(1)} %bitcast.11), channel_id=1, source_target_pairs={{0,64},{4,68},{8,72},{12,76},{16,80},{20,84},{24,88},{28,92},{32,9... | collective-permute-start | bytes 1769480 | tf_op jit(solution)/shard_map/ppermute | solution.py:18
  8.6 52.1 %collective-permute-start.1 = (f32[6,192,128]{2,1,0:T(8,128)S(1)}, f32[6,192,128]{2,1,0:T(8,128)S(1)}, u32[]{:S(2)}, u32[]{:S(2)}) collective-permute-start(f32[6,192,128]{2,1,0:T(8,128)S(1)} %bitcast.12), channel_id=1, source_target_pairs={{0,16},{4,20},{8,24},{12,28},{16,0},{20,4},{24,8},{28,12},{32,48},... | collective-permute-start | bytes 1769480 | tf_op jit(solution)/shard_map/ppermute | solution.py:18
  11.1 49.5 %collective-permute-start = (f32[6,192,128]{2,1,0:T(8,128)S(1)}, f32[6,192,128]{2,1,0:T(8,128)S(1)}, u32[]{:S(2)}, u32[]{:S(2)}) collective-permute-start(f32[6,192,128]{2,1,0:T(8,128)S(1)} %bitcast.13), channel_id=1, source_target_pairs={{0,8},{4,12},{8,0},{12,4},{16,24},{20,28},{24,16},{28,20},{32,40},... | collective-permute-start | bytes 1769480 | tf_op jit(solution)/shard_map/ppermute | solution.py:18

commit v2 on v0

v2 whole, which is shorter than its diff:
```python
import functools
import math

import jax
import jax.numpy as jnp
from jax import lax
from jax.experimental import pallas as pl
from jax.experimental.pallas import tpu as pltpu
from jax.sharding import PartitionSpec as P

DELTA2 = 0.05
BLK = 128
U = 48
KF = 48
STEPS = 3
PAD = 64


def from_partner(x, axis, stride):
    return lax.ppermute(x, axis, [(i, i ^ 1 << stride) for i in range(lax.axis_size(axis))])


def split3(v):
    h = v.astype(jnp.bfloat16).astype(jnp.float32)
    r = v - h
    m = r.astype(jnp.bfloat16).astype(jnp.float32)
    return h, m, r - m


def row(msg, c, nb, b):
    return jnp.broadcast_to(msg[pl.ds(c * nb + b, 1), :], (8, BLK))


def target_features(msg, nb, b, sub):
    x, y, z = row(msg, 0, nb, b), row(msg, 1, nb, b), row(msg, 2, nb, b)
    k = jnp.where(sub < 3, sub, sub - 3)
    v = jnp.where(k == 0, x, jnp.where(k == 1, y, z))
    h, m, l = split3(jnp.where(sub < 6, v, x * x + y * y + z * z + DELTA2))
    for_dist = jnp.where(sub < 3, -2.0, 0.0)
    for_num = jnp.where((sub >= 3) & (sub < 6), 1.0, 0.0)
    six = jnp.where(sub == 6, 1.0, 0.0)
    seven = jnp.where(sub == 7, -1.0, 0.0)
    dh, dm, dl = h * for_dist + six, m * for_dist, l * (for_dist + six)
    nh, nm, nl = h * for_num + seven, m * for_num, l * for_num
    dist = jnp.concatenate([dh, dh, dh, dm + h * six, dm + m * six, dl], axis=0)
    num = jnp.concatenate([nh, nh, nh, nm, nm, nl], axis=0)
    return jnp.concatenate([dist, num], axis=1).astype(jnp.bfloat16)


def source_features(msg, nb, b, sub):
    x, y, z = row(msg, 0, nb, b), row(msg, 1, nb, b), row(msg, 2, nb, b)
    u, v, w = row(msg, 3, nb, b), row(msg, 4, nb, b), row(msg, 5, nb, b)
    six = msg[pl.ds(b, 6, stride=nb), :]
    six = jnp.concatenate([six, jnp.zeros((2, BLK), jnp.float32)], axis=0)
    f = jnp.where(sub == 6, x * x + y * y + z * z, jnp.where(sub == 7, x * u + y * v + z * w, six))
    h, m, l = split3(f)
    hu = jnp.where(sub < 6, h, 1.0)
    mu = jnp.where(sub < 6, m, 1.0)
    return jnp.concatenate([h, m, l, hu, mu, hu], axis=0)


def phase_kernel(nb, rounds, own, last, lists, sizes, *refs):
    n_src = len(rounds) + (1 if own else 0)
    n_msg = n_src
    msgs, refs = refs[:n_msg], refs[n_msg:]
    if own:
        out, tgt, refs = refs[0], refs[1], refs[2:]
    else:
        before, tgt, out, refs = refs[0], refs[1], refs[2], refs[3:]
    even, odd, acc = refs
    src = (even, odd)
    width = 2 * nb + PAD
    ids = ([6] if own else []) + list(rounds)

    sub = lax.broadcasted_iota(jnp.int32, (8, BLK), 0)

    if own:
        acc[...] = jnp.zeros_like(acc)
        tgt[nb] = jnp.zeros((KF, 2 * BLK), jnp.bfloat16)
    else:
        acc[pl.ds(0, nb)] = before[...]

    def build(k, b):
        msg = msgs[k]
        f = source_features(msg, nb, b, sub)
        start = pl.multiple_of((k // 2 * nb + b) * BLK, BLK)
        src[k % 2][pl.ds(start, BLK), :KF] = f.astype(jnp.bfloat16).T
        if own and k == 0:
            tgt[b] = target_features(msg, nb, b, sub)

    def code_at(par, p):
        mine = ids[par::2]
        here = mine[0] * width + p
        if len(mine) > 1:
            size = sizes[mine[0]]
            here = jnp.where(p < size, here, mine[1] * width + (p - size))
        return lists[here]

    def tiles(par, at, ready, between):
        codes = []
        for u in range(U):
            code = code_at(par, at + u)
            codes.append(code if ready is None else jnp.where(ready, code, nb << 12))
        prods = []
        for code in codes:
            a = src[par][pl.ds(pl.multiple_of((code & 4095) * BLK, BLK), BLK), :KF]
            prods.append(jnp.dot(a, tgt[code >> 12], preferred_element_type=jnp.float32))
        between()
        for code, p in zip(codes, prods):
            s = lax.rsqrt(p[:, :BLK])
            w = p[:, BLK:] * (s * (s * s))
            acc[code >> 12] += jnp.sum(w.reshape(16, 8, BLK), axis=0)

    step = nb // STEPS

    def make(k, i):
        for j in range(step):
            build(k, i * step + j)

    def first(i, _):
        make(0, i)
        return 0

    lax.fori_loop(0, STEPS, first, 0)
    found = [sizes[ids[0]], jnp.int32(0)]
    done = [jnp.int32(0), jnp.int32(0)]
    for k in range(1, n_src):
        par = (k - 1) % 2

        def both(i, at, k=k, par=par, have=found[par]):
            ready = at + U <= have
            tiles(par, at, ready, lambda: make(k, i))
            return jnp.where(ready, at + U, at)

        done[par] = lax.fori_loop(0, STEPS, both, done[par])
        found[k % 2] += sizes[ids[k]]

    for par in range(min(2, n_src)):

        def rest(i, at, par=par):
            tiles(par, at, None, lambda: None)
            return at + U

        lax.fori_loop(0, (found[par] - done[par] + U - 1) // U, rest, done[par])

    if last:

        def finish(i, _):
            out[pl.ds(pl.multiple_of(i * 8, 8), 8), :] = jnp.sum(acc[pl.ds(i * 8, 8)], axis=1)
            return 0

        lax.fori_loop(0, nb // 8, finish, 0)
    else:
        out[...] = acc[pl.ds(0, nb)]


def phase(name, rounds, own, last, lists, sizes, msgs, before):
    nb = msgs[0].shape[0] // 6
    n_src = len(msgs)
    smem, vmem = pl.BlockSpec(memory_space=pltpu.SMEM), pl.BlockSpec(memory_space=pltpu.VMEM)
    args = [lists, sizes, *msgs, *before]
    shapes = [jax.ShapeDtypeStruct((nb, BLK) if last else (nb, 8, BLK), jnp.float32)]
    if own:
        shapes.append(jax.ShapeDtypeStruct((nb + 1, KF, 2 * BLK), jnp.bfloat16))
    return pl.pallas_call(
        functools.partial(phase_kernel, nb, tuple(rounds), own, last),
        out_shape=shapes,
        in_specs=[smem, smem] + [vmem] * (len(args) - 2),
        out_specs=[vmem] * len(shapes),
        scratch_shapes=[
            pltpu.VMEM(((n_src + 1) // 2 * nb * BLK, BLK), jnp.bfloat16),
            pltpu.VMEM((n_src // 2 * nb * BLK, BLK), jnp.bfloat16),
            pltpu.VMEM((nb + 1, 8, BLK), jnp.float32),
        ],
        compiler_params=pltpu.CompilerParams(vmem_limit_bytes=40 << 20),
        cost_estimate=pl.CostEstimate(flops=n_src * 2_000_000_000, bytes_accessed=n_src * 1_000_000, transcendentals=0),
        name=name,
    )(*args)


def tile_lists(near_index, near_count):
    nb, rounds, slots = near_index.shape
    width = slots * nb + PAD
    half = [0, 0, 1, 0, 0, 0]
    t = jnp.arange(nb, dtype=jnp.int32)
    place = jnp.arange(width, dtype=jnp.int32)
    count = near_count.T
    index = near_index.transpose(1, 2, 0)
    before = jnp.sum(jnp.where(t[:, None] < t[None, :], count[:, :, None], 0), axis=1)
    size = jnp.sum(count, axis=1)
    lists = jnp.where(place[None] < size[:, None], 0, nb << 12)
    for s in range(slots):
        code = index[:, s] + (t << 12) + (jnp.array(half, jnp.int32) * nb)[:, None]
        at = jnp.where(s < count, before + s, -1)
        lists += jnp.sum(jnp.where(at[:, :, None] == place, code[:, :, None], 0), axis=1)
    own = jnp.where(place < nb, (place << 12) + place, nb << 12)
    lists = jnp.concatenate([lists, own[None]], axis=0).reshape(-1)
    return lists, jnp.concatenate([size, jnp.full((1,), nb, jnp.int32)])


def shards(positions, normals, strength, near_index, near_count):
    nb = near_index.shape[0]
    scaled = normals * (strength * (1.0 / (4.0 * math.pi)))[None]
    mine = jnp.concatenate([positions, scaled], axis=0).reshape(6 * nb, BLK)
    top_bit = lax.axis_size("bulk").bit_length() - 2
    plan = [("grp", 0), ("grp", 1), ("bulk", 0), ("bulk", 1), ("bulk", 2), ("bulk", top_bit)]
    far = [from_partner(mine, axis, bit) for axis, bit in plan]
    lists, sizes = tile_lists(near_index, near_count)
    a, tgt = phase("own_core", [0], True, False, lists, sizes, [mine, far[0]], [])
    (b,) = phase("mid", [5, 1, 2], False, False, lists, sizes, [far[5], far[1], far[2]], [a, tgt])
    (c,) = phase("end", [3, 4], False, True, lists, sizes, [far[3], far[4]], [b, tgt])
    return c.reshape(-1)


def solution(mesh):
    in_specs = (
        P(None, ("bulk", "grp")),
        P(None, ("bulk", "grp")),
        P(("bulk", "grp")),
        P(("bulk", "grp"), None, None),
        P(("bulk", "grp"), None),
    )
    out_specs = P(("bulk", "grp"))
    return jax.shard_map(shards, mesh=mesh, in_specs=in_specs, out_specs=out_specs, check_vma=False)
```

time: 521 us -> 66.7 us (0.13); the launches traced: 513 us -> 65.4 us
  matrix products: 408 us -> 0 us
  local copies, waits for them, and re-layouts: 56 us -> 1.9 us
  Pallas kernels: 0 us -> 43.1 us
  starting transfers between devices: 28.1 us -> 12.8 us
  other arithmetic: 18.4 us -> 7.4 us
    dot_general x7 -> x0, matrix products: 408 us -> none  [tile_sum(): jnp.einsum('tkij,tkj->tki', kernel, src_q, precision=high)]
    pallas_call x0 -> x3, Pallas kernels: none -> 43.1 us  [phase(): pl.pallas_call(functools.partial(phase_kernel, nb, tuple(rounds), own, la...]
    gather x18 -> x0, local copies, waits for them, and re-layouts: 37.2 us -> none  [the longest x6 14.1 us: near_terms(): chosen_pos = pos_blocks[:, index_round]]
    slice x15 -> x1, local copies, waits for them, and re-layouts: 16.8 us -> 0.8 us  [tile_lists(): code = index[:, s] + (t << 12) + (jnp.array(half, jnp.int32) * nb)[:, None]]
    ppermute x18 -> x6, starting transfers between devices: 28.1 us -> 12.8 us  [from_partner(): lax.ppermute(x, axis, [(i, i ^ 1 << stride) for i in range(lax.axis_size(...]
    reduce_sum x10 -> x3, other arithmetic: 14.3 us -> 1.97 us  [the longest x1 1.62 us: tile_lists(): jnp.sum(jnp.where(at[:, :, None] == place, code[:, :, None], 0), axis=1)]
  transfers between devices with their start and end apart: 18 -> 6, of which waited for: 0 -> 0; matrix products, arithmetic and copies ran while one was open for 20% -> 9% of each run, Pallas kernels for 0% -> 45%
where the time goes in v2:
time: 66.7 us; the launch traced here: 65.4 us
  Pallas kernels  43.1 us (65%)
  starting transfers between devices  12.8 us (19%)
  other arithmetic  7.4 us (11%)
  local copies, waits for them, and re-layouts  1.9 us (3%)
    pallas_call x3, Pallas kernels, phase(): pl.pallas_call(functools.partial(phase_kernel, nb, tuple(rounds), own, la...  43.1 us
    ppermute x6, starting transfers between devices, from_partner(): lax.ppermute(x, axis, [(i, i ^ 1 << stride) for i in range(lax.axis_size(...  12.8 us
    mul x2, other arithmetic, shards(): scaled = normals * (strength * (1.0 / (4.0 * math.pi)))[None]  2.03 us
    reduce_sum x1, other arithmetic, tile_lists(): jnp.sum(jnp.where(at[:, :, None] == place, code[:, :, None], 0), axis=1)  1.62 us
  transfers between devices with their start and end apart: 6, of which 0 were waited for; matrix products, arithmetic and copies ran while one was open for 9% of the time, Pallas kernels for 45%

profile of v2, /device:TPU:0, one launch (start us, length us, event | category | flops | bytes accessed | tf_op | source)
XLA Modules:
  0.0 65.4 jit_solution(9056431185282459526)
XLA Ops:
  0.0 0.0 copy-start.2
  0.0 0.0 copy-start
  0.0 0.9 %broadcast_multiply_fusion.1 = f32[24576]{0:T(1024)S(1)} fusion(f32[24576]{0:T(1024)} %param.9), kind=kLoop, calls=%fused_computation.8 | loop fusion | flops 24576 | bytes 196608 | tf_op jit(solution)/shard_map/mul | solution.py:203
  0.9 1.1 %broadcast_multiply_fusion = f32[3,24576]{1,0:T(4,128)S(1)} fusion(f32[3,24576]{1,0:T(4,128)} %param.8, f32[24576]{0:T(1024)S(1)} %broadcast_multiply_fusion.1), kind=kLoop, calls=%fused_computation.6 | loop fusion | flops 73728 | bytes 688128 | tf_op jit(solution)/shard_map/mul | solution.py:203
  2.0 1.2 %pad_maximum_fusion = f32[6,24576]{1,0:T(8,128)S(1)} fusion(f32[3,24576]{1,0:T(4,128)S(1)} %broadcast_multiply_fusion, f32[3,24576]{1,0:T(4,128)} %param.7), kind=kLoop, calls=%fused_computation.5 | loop fusion | flops 147456 | bytes 1179648 | tf_op jit(solution)/shard_map/concatenate | solution.py:204
  3.2 0.3 reshape.107.refs_0_
  3.5 0.1 collective-permute-start.5
  3.6 4.0 %collective-permute-start.2 = (f32[1152,128]{1,0:T(8,128)S(1)}, f32[1152,128]{1,0:T(8,128)S(1)}, u32[]{:S(2)}, u32[]{:S(2)}) collective-permute-start(f32[1152,128]{1,0:T(8,128)S(1)} %reshape.107.refs_0_), channel_id=1, source_target_pairs={{0,64},{4,68},{8,72},{12,76},{16,80},{20,84},{24,88},{28,92},{32,9... | collective-permute-start | bytes 1769480 | tf_op jit(solution)/shard_map/ppermute | solution.py:20
  7.7 1.5 %collective-permute-start.3 = (f32[1152,128]{1,0:T(8,128)S(1)}, f32[1152,128]{1,0:T(8,128)S(1)}, u32[]{:S(2)}, u32[]{:S(2)}) collective-permute-start(f32[1152,128]{1,0:T(8,128)S(1)} %reshape.107.refs_0_), channel_id=1, source_target_pairs={{0,2},{1,3},{2,0},{3,1},{4,6},{5,7},{6,4},{7,5},{8,10},{9,11},{10,... | collective-permute-start | bytes 1769480 | tf_op jit(solution)/shard_map/ppermute | solution.py:20
  9.1 1.6 %collective-permute-start.4 = (f32[1152,128]{1,0:T(8,128)S(1)}, f32[1152,128]{1,0:T(8,128)S(1)}, u32[]{:S(2)}, u32[]{:S(2)}) collective-permute-start(f32[1152,128]{1,0:T(8,128)S(1)} %reshape.107.refs_0_), channel_id=1, source_target_pairs={{0,4},{4,0},{8,12},{12,8},{16,20},{20,16},{24,28},{28,24},{32,36},... | collective-permute-start | bytes 1769480 | tf_op jit(solution)/shard_map/ppermute | solution.py:20
  10.7 2.9 %collective-permute-start = (f32[1152,128]{1,0:T(8,128)S(1)}, f32[1152,128]{1,0:T(8,128)S(1)}, u32[]{:S(2)}, u32[]{:S(2)}) collective-permute-start(f32[1152,128]{1,0:T(8,128)S(1)} %reshape.107.refs_0_), channel_id=1, source_target_pairs={{0,8},{4,12},{8,0},{12,4},{16,24},{20,28},{24,16},{28,20},{32,40},... | collective-permute-start | bytes 1769480 | tf_op jit(solution)/shard_map/ppermute | solution.py:20
  13.6 0.8 %fusion.3 = (s32[6,1,192]{2,1,0:T(1,128)S(1)}, s32[6,1,192]{2,1,0:T(1,128)S(1)}) fusion(s32[6,2,192]{2,1,0:T(2,128)} %bitcast.16), kind=kLoop, calls=%fused_computation.24 | loop fusion | bytes 18432 | tf_op jit(solution)/shard_map/slice | solution.py:193
  14.4 0.0 copy-done
  14.5 0.2 select_reduce_fusion.2
  14.7 0.0 copy-done.2
  14.7 0.1 fusion.1
  14.8 1.6 %select_reduce_fusion = (s32[6,448]{1,0:T(8,128)}, s32[6,448]{1,0:T(8,128)}) fusion(s32[6,192]{1,0:T(8,128)S(1)} %get-tuple-element.14, s32[6,192]{1,0:T(8,128)S(1)} %get-tuple-element.10, s32[6,192]{1,0:T(8,128)S(1)} %get-tuple-element.13, s32[6,192]{1,0:T(8,128)S(1)} %get-tuple-element.9), kind=kLoop, calls=%fused_computation | loop fusion | flops 3091200 | bytes 39936 | tf_op jit(solution)/shard_map/reduce_sum | solution.py:195
  16.4 0.1 reduce_sum.36
  16.5 0.0 copy-start.1
  16.5 0.8 %add_add_fusion = s32[6,448]{1,0:T(8,128)S(1)} fusion(s32[6,448]{1,0:T(8,128)} %get-tuple-element.15, s32[6,448]{1,0:T(8,128)} %get-tuple-element.16, s32[6]{0:T(128)S(1)} %reduce_sum.36), kind=kLoop, calls=%fused_computation.10 | loop fusion | flops 10752 | bytes 32280 | tf_op jit(solution)/shard_map/add | solution.py:195
  17.4 0.0 copy-done.1
  17.4 0.6 pad_add_fusion
  18.0 0.8 %reshape.106.lists = s32[3136]{0:T(1024)S(1)} reshape(s32[7,448]{1,0:T(8,128)} %pad_add_fusion) | data formatting | bytes 25088 | tf_op jit(solution)/shard_map/reshape | solution.py:197
  18.8 0.7 %pad_add_fusion.1.sizes = s32[7]{0:T(128)S(1)} fusion(s32[1]{0:T(128)} %constant.4.clone.1, s32[6]{0:T(128)} %copy-done.1), kind=kLoop, calls=%fused_computation.23 | loop fusion | flops 7 | bytes 56 | tf_op jit(solution)/shard_map/concatenate | solution.py:198
  19.5 0.0 collective-permute-done.5.refs_1_
  19.5 2.7 %collective-permute-start.1 = (f32[1152,128]{1,0:T(8,128)S(1)}, f32[1152,128]{1,0:T(8,128)S(1)}, u32[]{:S(2)}, u32[]{:S(2)}) collective-permute-start(f32[1152,128]{1,0:T(8,128)S(1)} %reshape.107.refs_0_), channel_id=1, source_target_pairs={{0,16},{4,20},{8,24},{12,28},{16,0},{20,4},{24,8},{28,12},{32,48},... | collective-permute-start | bytes 1769480 | tf_op jit(solution)/shard_map/ppermute | solution.py:20
  22.2 12.2 %own_core.1 = (f32[192,8,128]{2,1,0:T(8,128)S(1)}, bf16[193,48,256]{2,1,0:T(8,128)(2,1)S(1)}) custom-call(s32[3136]{0:T(1024)S(1)} %reshape.106.lists, s32[7]{0:T(128)S(1)} %pad_add_fusion.1.sizes, f32[1152,128]{1,0:T(8,128)S(1)} %reshape.107.refs_0_, f32[1152,128]{1,0:T(8,128)S(1)} %collective-permute-done.5.refs_1_), custom_call_target="tpu_custom_call" | custom-call | flops 4000000000 | bytes 2000000 | tf_op jit(solution)/shard_map/own_core/pallas_call | solution.py:165
  34.4 0.0 collective-permute-done.2.refs_0_
  34.5 0.0 collective-permute-done.3.refs_1_
  34.5 0.0 collective-permute-done.4.refs_2_
  34.5 17.4 %mid.1.refs_2_ = f32[192,8,128]{2,1,0:T(8,128)S(1)} custom-call(s32[3136]{0:T(1024)S(1)} %reshape.106.lists, s32[7]{0:T(128)S(1)} %pad_add_fusion.1.sizes, f32[1152,128]{1,0:T(8,128)S(1)} %collective-permute-done.2.refs_0_, f32[1152,128]{1,0:T(8,128)S(1)} %collective-permute-done.3.refs_1_, f32[1152,128]{1,0:T(8,128)S(1)} %collective-permute-done.4.refs_2_, ...), custom_call_target="tpu_custom_call" | custom-call | flops 6000000000 | bytes 3000000 | tf_op jit(solution)/shard_map/mid/pallas_call | solution.py:165
  51.9 0.0 collective-permute-done.refs_0_
  51.9 0.0 collective-permute-done.1.refs_1_
  51.9 13.5 %end.1 = f32[192,128]{1,0:T(8,128)} custom-call(s32[3136]{0:T(1024)S(1)} %reshape.106.lists, s32[7]{0:T(128)S(1)} %pad_add_fusion.1.sizes, f32[1152,128]{1,0:T(8,128)S(1)} %collective-permute-done.refs_0_, f32[1152,128]{1,0:T(8,128)S(1)} %collective-permute-done.1.refs_1_, f32[192,8,128]{2,1,0:T(8,128)S(1)} %mid.1.refs_2_, ...), custom_call_target="tpu_custom_call" | custom-call | flops 4000000000 | bytes 2000000 | tf_op jit(solution)/shard_map/end/pallas_call | solution.py:165
  (4 shorter events, 0.0 us)
Async XLA Ops:
  0.0 14.7 %copy-start.2 = (s32[6]{0:T(128)S(1)}, s32[6]{0:T(128)}, u32[]{:S(2)}) copy-start(s32[6]{0:T(128)} %constant.24) | copy-start | bytes 76
  0.0 14.4 %copy-start = (s32[192,6]{0,1:T(8,128)S(1)}, s32[192,6]{0,1:T(8,128)}, u32[]{:S(2)}) copy-start(s32[192,6]{0,1:T(8,128)} %param.11) | copy-start | bytes 13828
  3.5 16.0 %collective-permute-start.5 = (f32[1152,128]{1,0:T(8,128)S(1)}, f32[1152,128]{1,0:T(8,128)S(1)}, u32[]{:S(2)}, u32[]{:S(2)}) collective-permute-start(f32[1152,128]{1,0:T(8,128)S(1)} %reshape.107.refs_0_), channel_id=1, source_target_pairs={{0,1},{1,0},{2,3},{3,2},{4,5},{5,4},{6,7},{7,6},{8,9},{9,8},{10,11... | collective-permute-start | bytes 1769480 | tf_op jit(solution)/shard_map/ppermute | solution.py:20
  3.6 30.8 %collective-permute-start.2 = (f32[1152,128]{1,0:T(8,128)S(1)}, f32[1152,128]{1,0:T(8,128)S(1)}, u32[]{:S(2)}, u32[]{:S(2)}) collective-permute-start(f32[1152,128]{1,0:T(8,128)S(1)} %reshape.107.refs_0_), channel_id=1, source_target_pairs={{0,64},{4,68},{8,72},{12,76},{16,80},{20,84},{24,88},{28,92},{32,9... | collective-permute-start | bytes 1769480 | tf_op jit(solution)/shard_map/ppermute | solution.py:20
  7.7 26.8 %collective-permute-start.3 = (f32[1152,128]{1,0:T(8,128)S(1)}, f32[1152,128]{1,0:T(8,128)S(1)}, u32[]{:S(2)}, u32[]{:S(2)}) collective-permute-start(f32[1152,128]{1,0:T(8,128)S(1)} %reshape.107.refs_0_), channel_id=1, source_target_pairs={{0,2},{1,3},{2,0},{3,1},{4,6},{5,7},{6,4},{7,5},{8,10},{9,11},{10,... | collective-permute-start | bytes 1769480 | tf_op jit(solution)/shard_map/ppermute | solution.py:20
  9.1 25.3 %collective-permute-start.4 = (f32[1152,128]{1,0:T(8,128)S(1)}, f32[1152,128]{1,0:T(8,128)S(1)}, u32[]{:S(2)}, u32[]{:S(2)}) collective-permute-start(f32[1152,128]{1,0:T(8,128)S(1)} %reshape.107.refs_0_), channel_id=1, source_target_pairs={{0,4},{4,0},{8,12},{12,8},{16,20},{20,16},{24,28},{28,24},{32,36},... | collective-permute-start | bytes 1769480 | tf_op jit(solution)/shard_map/ppermute | solution.py:20
  10.7 41.2 %collective-permute-start = (f32[1152,128]{1,0:T(8,128)S(1)}, f32[1152,128]{1,0:T(8,128)S(1)}, u32[]{:S(2)}, u32[]{:S(2)}) collective-permute-start(f32[1152,128]{1,0:T(8,128)S(1)} %reshape.107.refs_0_), channel_id=1, source_target_pairs={{0,8},{4,12},{8,0},{12,4},{16,24},{20,28},{24,16},{28,20},{32,40},... | collective-permute-start | bytes 1769480 | tf_op jit(solution)/shard_map/ppermute | solution.py:20
  16.5 0.8 %copy-start.1 = (s32[6]{0:T(128)}, s32[6]{0:T(128)S(1)}, u32[]{:S(2)}) copy-start(s32[6]{0:T(128)S(1)} %reduce_sum.36) | copy-start | bytes 76
  19.5 32.4 %collective-permute-start.1 = (f32[1152,128]{1,0:T(8,128)S(1)}, f32[1152,128]{1,0:T(8,128)S(1)}, u32[]{:S(2)}, u32[]{:S(2)}) collective-permute-start(f32[1152,128]{1,0:T(8,128)S(1)} %reshape.107.refs_0_), channel_id=1, source_target_pairs={{0,16},{4,20},{8,24},{12,28},{16,0},{20,4},{24,8},{28,12},{32,48},... | collective-permute-start | bytes 1769480 | tf_op jit(solution)/shard_map/ppermute | solution.py:20

commit v3 on v2

v3 whole, which is shorter than its diff:
```python
import functools
import math

import jax
import jax.numpy as jnp
from jax import lax
from jax.experimental import pallas as pl
from jax.experimental.pallas import tpu as pltpu
from jax.sharding import PartitionSpec as P

DELTA2 = 0.05
BLK = 128
U = 48
KF = 48
STEPS = 3
PAD = 128
OWN = 6


def from_partner(x, axis, stride):
    return lax.ppermute(x, axis, [(i, i ^ 1 << stride) for i in range(lax.axis_size(axis))])


def split3(v):
    h = v.astype(jnp.bfloat16).astype(jnp.float32)
    r = v - h
    m = r.astype(jnp.bfloat16).astype(jnp.float32)
    return h, m, r - m


def row(msg, c, nb, b):
    return jnp.broadcast_to(msg[pl.ds(c * nb + b, 1), :], (8, BLK))


def target_features(msg, nb, b, sub):
    x, y, z = row(msg, 0, nb, b), row(msg, 1, nb, b), row(msg, 2, nb, b)
    k = jnp.where(sub < 3, sub, sub - 3)
    v = jnp.where(k == 0, x, jnp.where(k == 1, y, z))
    h, m, l = split3(jnp.where(sub < 6, v, x * x + y * y + z * z + DELTA2))
    for_dist = jnp.where(sub < 3, -2.0, 0.0)
    for_num = jnp.where((sub >= 3) & (sub < 6), 1.0, 0.0)
    six = jnp.where(sub == 6, 1.0, 0.0)
    seven = jnp.where(sub == 7, -1.0, 0.0)
    dh, dm, dl = h * for_dist + six, m * for_dist, l * (for_dist + six)
    nh, nm, nl = h * for_num + seven, m * for_num, l * for_num
    dist = jnp.concatenate([dh, dh, dh, dm + h * six, dm + m * six, dl], axis=0)
    num = jnp.concatenate([nh, nh, nh, nm, nm, nl], axis=0)
    return jnp.concatenate([dist, num], axis=1).astype(jnp.bfloat16)


def source_features(msg, nb, b, sub):
    x, y, z = row(msg, 0, nb, b), row(msg, 1, nb, b), row(msg, 2, nb, b)
    u, v, w = row(msg, 3, nb, b), row(msg, 4, nb, b), row(msg, 5, nb, b)
    six = msg[pl.ds(b, 6, stride=nb), :]
    six = jnp.concatenate([six, jnp.zeros((2, BLK), jnp.float32)], axis=0)
    f = jnp.where(sub == 6, x * x + y * y + z * z, jnp.where(sub == 7, x * u + y * v + z * w, six))
    h, m, l = split3(f)
    hu = jnp.where(sub < 6, h, 1.0)
    mu = jnp.where(sub < 6, m, 1.0)
    return jnp.concatenate([h, m, l, hu, mu, hu], axis=0)


def phase_kernel(nb, chain, carry_in, carry_out, last, lists, *refs):
    own = not carry_in
    n = len(chain)
    n_msg = n - (1 if carry_in else 0)
    msgs, refs = refs[:n_msg], refs[n_msg:]
    if own:
        out, tgt, refs = refs[0], refs[1], refs[2:]
    else:
        before, tgt, src_in, out, refs = refs[0], refs[1], refs[2], refs[3], refs[4:]
    if carry_out:
        src_out, refs = refs[0], refs[1:]
    acc, kept = refs[0], list(refs[1:])
    src = ([src_in] if carry_in else []) + kept + ([src_out] if carry_out else [])
    width = 2 * nb + PAD
    sizes = [lists[7 * width + i] for i in chain]
    sub = lax.broadcasted_iota(jnp.int32, (8, BLK), 0)

    if own:
        acc[...] = jnp.zeros_like(acc)
        tgt[nb] = jnp.zeros((KF, 2 * BLK), jnp.bfloat16)
    else:
        acc[pl.ds(0, nb)] = before[...]

    step = nb // STEPS

    def make(k, i):
        msg = msgs[k - (1 if carry_in else 0)]
        for j in range(step):
            b = i * step + j
            f = source_features(msg, nb, b, sub)
            src[k][pl.ds(pl.multiple_of(b * BLK, BLK), BLK), :KF] = f.astype(jnp.bfloat16).T
            if chain[k] == OWN:
                tgt[b] = target_features(msg, nb, b, sub)

    def tiles(slots, between):
        codes, prods = [], []
        for k, p in slots:
            codes.append(lists[chain[k] * width + p])
        for (k, _), code in zip(slots, codes):
            a = src[k][pl.ds(pl.multiple_of((code & 255) * BLK, BLK), BLK), :KF]
            prods.append(jnp.dot(a, tgt[code >> 12], preferred_element_type=jnp.float32))
        between()
        for code, p in zip(codes, prods):
            s = lax.rsqrt(p[:, :BLK])
            w = p[:, BLK:] * (s * (s * s))
            acc[code >> 12] += jnp.sum(w.reshape(16, 8, BLK), axis=0)

    if own:

        def first(i, _):
            make(0, i)
            return 0

        lax.fori_loop(0, STEPS, first, 0)

    done = [jnp.int32(0)] * n
    for k in range(1, n):

        def both(i, at, k=k):
            ready = at + U <= sizes[k - 1]
            at_or_none = jnp.where(ready, at, width - U)
            tiles([(k - 1, at_or_none + u) for u in range(U)], lambda: make(k, i))
            return jnp.where(ready, at + U, at)

        done[k - 1] = lax.fori_loop(0, STEPS, both, done[k - 1])

    groups = [list(range(n - 1))] + ([] if carry_out else [[n - 1]])
    for group in groups:
        each = U // len(group)
        todo = jnp.int32(0)
        for k in group:
            todo = jnp.maximum(todo, (sizes[k] - done[k] + each - 1) // each)

        def rest(i, at, group=group, each=each):
            slots = [(k, jnp.minimum(p + u, width - 1)) for k, p in zip(group, at) for u in range(each)]
            tiles(slots, lambda: None)
            return tuple(p + each for p in at)

        lax.fori_loop(0, todo, rest, tuple(done[k] for k in group))

    if last:

        def finish(i, _):
            out[pl.ds(pl.multiple_of(i * 8, 8), 8), :] = jnp.sum(acc[pl.ds(i * 8, 8)], axis=1)
            return 0

        lax.fori_loop(0, nb // 8, finish, 0, unroll=4)
    else:
        out[...] = acc[pl.ds(0, nb)]


def phase(name, chain, lists, msgs, before, carry_out):
    nb = msgs[0].shape[0] // 6
    carry_in = len(before) > 0
    last = not carry_out
    smem, vmem = pl.BlockSpec(memory_space=pltpu.SMEM), pl.BlockSpec(memory_space=pltpu.VMEM)
    args = [lists, *msgs, *before]
    shapes = [jax.ShapeDtypeStruct((nb, BLK) if last else (nb, 8, BLK), jnp.float32)]
    if not carry_in:
        shapes.append(jax.ShapeDtypeStruct((nb + 1, KF, 2 * BLK), jnp.bfloat16))
    if carry_out:
        shapes.append(jax.ShapeDtypeStruct((nb * BLK, BLK), jnp.bfloat16))
    kept = len(chain) - (1 if carry_in else 0) - (1 if carry_out else 0)
    return pl.pallas_call(
        functools.partial(phase_kernel, nb, tuple(chain), carry_in, carry_out, last),
        out_shape=shapes,
        in_specs=[smem] + [vmem] * (len(args) - 1),
        out_specs=[vmem] * len(shapes),
        scratch_shapes=[pltpu.VMEM((nb + 1, 8, BLK), jnp.float32)] + [pltpu.VMEM((nb * BLK, BLK), jnp.bfloat16)] * kept,
        compiler_params=pltpu.CompilerParams(vmem_limit_bytes=26 << 20),
        cost_estimate=pl.CostEstimate(
            flops=len(chain) * 2_000_000_000, bytes_accessed=len(chain) * 1_000_000, transcendentals=0
        ),
        name=name,
    )(*args)


def start_kernel(nb, rounds, *refs):
    outside, (msg, lists), inside, sems = refs[:5], refs[5:7], refs[7:12], refs[12]
    copies = [pltpu.make_async_copy(o, i, sems.at[n]) for n, (o, i) in enumerate(zip(outside, inside))]
    for copy in copies[::-1]:
        copy.start()
    pos, nrm, dens, index, count = inside

    def plane(i, _):
        for j in range(8):
            b = i * 8 + j
            at = pl.ds(pl.multiple_of(b * BLK, BLK), BLK)
            msg[pl.ds(b, 3, stride=nb), :] = pos[:, at]
            q = dens[pl.ds(b, 1), :] * (1.0 / (4.0 * math.pi))
            msg[pl.ds(3 * nb + b, 3, stride=nb), :] = nrm[:, at] * q
        return 0

    copies[4].wait()
    copies[3].wait()
    width = 2 * nb + PAD
    slots = index.shape[1]
    c = count[...]
    t_row = lax.broadcasted_iota(jnp.int32, (nb, nb), 0)
    t_col = lax.broadcasted_iota(jnp.int32, (nb, nb), 1)
    earlier = jnp.where(t_row < t_col, 1.0, 0.0).astype(jnp.bfloat16)
    pad = jnp.zeros((16 - rounds, nb), jnp.float32)
    cf = jnp.concatenate([c.astype(jnp.float32), pad], axis=0)
    before = jnp.dot(cf.astype(jnp.bfloat16), earlier, preferred_element_type=jnp.float32)
    size = jnp.sum(cf, axis=1, keepdims=True)
    place = lax.broadcasted_iota(jnp.int32, (1, width), 1)
    spot = lax.broadcasted_iota(jnp.int32, (width, nb), 0).astype(jnp.float32)
    t = lax.broadcasted_iota(jnp.int32, (1, nb), 1).astype(jnp.float32)
    rest = jnp.zeros((14, nb), jnp.float32)
    rows = []
    for r in range(rounds):
        both = jnp.zeros((16, width), jnp.float32)
        for s in range(slots):
            at = jnp.where(cf[r:r + 1] > s, before[r:r + 1] + s, -1.0)
            hot = jnp.where(spot == at, 1.0, 0.0).astype(jnp.bfloat16)
            code = jnp.concatenate([index[r, pl.ds(s, 1), :].astype(jnp.float32), t, rest], axis=0)
            both += lax.dot_general(
                code.astype(jnp.bfloat16), hot, (((1,), (1,)), ((), ())), preferred_element_type=jnp.float32
            )
        row = (both[1:2] * 4096.0 + both[0:1]).astype(jnp.int32)
        rows.append(jnp.where(place.astype(jnp.float32) < size[r:r + 1], row, nb << 12))
    rows.append(jnp.where(place < nb, (place << 12) + place, nb << 12))
    sub = lax.broadcasted_iota(jnp.int32, (16, BLK), 0)
    lane = lax.broadcasted_iota(jnp.int32, (16, BLK), 1)
    sizes = jnp.sum(jnp.where(sub == lane, size, 0.0), axis=0, keepdims=True)
    sizes = jnp.where(lane[:1] == rounds, float(nb), sizes).astype(jnp.int32)
    parts = width // BLK
    for i, row in enumerate(rows):
        for q in range(parts):
            lists[pl.ds(i * parts + q, 1), :] = row[:, q * BLK:(q + 1) * BLK]
    lists[pl.ds(len(rows) * parts, 1), :] = sizes
    for copy in copies[:3]:
        copy.wait()
    lax.fori_loop(0, nb // 8, plane, 0)


def start(positions, normals, strength, near_index, near_count):
    nb, rounds, slots = near_index.shape
    rows = (rounds + 2) * (slots * nb + PAD) // BLK
    vmem = pl.BlockSpec(memory_space=pltpu.VMEM)
    index = near_index.transpose(1, 2, 0)
    args = [positions, normals, strength.reshape(nb, BLK), index, near_count.T]
    msg, lists = pl.pallas_call(
        functools.partial(start_kernel, nb, rounds),
        out_shape=[
            jax.ShapeDtypeStruct((6 * nb, BLK), jnp.float32),
            jax.ShapeDtypeStruct((rows, BLK), jnp.int32),
        ],
        in_specs=[pl.BlockSpec(memory_space=pltpu.HBM)] * 5,
        out_specs=[vmem] * 2,
        scratch_shapes=[pltpu.VMEM(a.shape, a.dtype) for a in args] + [pltpu.SemaphoreType.DMA((5,))],
        compiler_params=pltpu.CompilerParams(vmem_limit_bytes=24 << 20),
        name="start",
    )(*[pltpu.with_memory_space_constraint(a, pltpu.HBM) for a in args])
    return msg, lists.reshape(-1)


def shards(positions, normals, strength, near_index, near_count):
    mine, lists = start(positions, normals, strength, near_index, near_count)
    top_bit = lax.axis_size("bulk").bit_length() - 2
    plan = [("grp", 0), ("grp", 1), ("bulk", 0), ("bulk", 1), ("bulk", 2), ("bulk", top_bit)]
    far = [from_partner(mine, axis, bit) for axis, bit in plan]
    a, tgt, held = phase("own_core", [OWN, 0], lists, [mine, far[0]], [], True)
    b, held = phase("mid", [0, 5, 1, 2], lists, [far[5], far[1], far[2]], [a, tgt, held], True)
    (c,) = phase("end", [2, 3, 4], lists, [far[3], far[4]], [b, tgt, held], False)
    return c.reshape(-1)


def solution(mesh):
    in_specs = (
        P(None, ("bulk", "grp")),
        P(None, ("bulk", "grp")),
        P(("bulk", "grp")),
        P(("bulk", "grp"), None, None),
        P(("bulk", "grp"), None),
    )
    out_specs = P(("bulk", "grp"))
    return jax.shard_map(shards, mesh=mesh, in_specs=in_specs, out_specs=out_specs, check_vma=False)
```

time: 66.7 us -> 59.1 us (0.89)
  other arithmetic: 7.4 us -> 0 us
  local copies, waits for them, and re-layouts: 1.9 us -> 0 us
  Pallas kernels: 43.1 us -> 44.6 us
    concatenate x3 -> x0, other arithmetic: 2.48 us -> none  [the longest x1 1.16 us: shards(): mine = jnp.concatenate([positions, scaled], axis=0).reshape(6 * nb, BLK)]
    mul x2 -> x0, other arithmetic: 2.03 us -> none  [shards(): scaled = normals * (strength * (1.0 / (4.0 * math.pi)))[None]]
    reduce_sum x3 -> x0, other arithmetic: 1.97 us -> none  [the longest x1 1.62 us: tile_lists(): jnp.sum(jnp.where(at[:, :, None] == place, code[:, :, None], 0), axis=1)]
    pallas_call x3 -> x4, Pallas kernels: 43.1 us -> 44.6 us  [the longest x3 42.1 us: phase(): pl.pallas_call(functools.partial(phase_kernel, nb, tuple(chain), carry_in...]
    reshape x2 -> x0, local copies, waits for them, and re-layouts: 1.1 us -> none  [the longest x1 0.79 us: tile_lists(): lists = jnp.concatenate([lists, own[None]], axis=0).reshape(-1)]
    add x2 -> x0, other arithmetic: 0.88 us -> none  [the longest x1 0.81 us: tile_lists(): lists += jnp.sum(jnp.where(at[:, :, None] == place, code[:, :, None], 0),...]
    slice x1 -> x0, local copies, waits for them, and re-layouts: 0.8 us -> none  [tile_lists(): code = index[:, s] + (t << 12) + (jnp.array(half, jnp.int32) * nb)[:, None]]
    ppermute x6, waiting for transfers between devices: 0.02 us -> 0.68 us  [from_partner(): lax.ppermute(x, axis, [(i, i ^ 1 << stride) for i in range(lax.axis_size(...]
  transfers between devices with their start and end apart: 6 -> 6, of which waited for: 0 -> 1; matrix products, arithmetic and copies ran while one was open for 9% -> 0% of each run, Pallas kernels for 45% -> 43%
where the time goes in v3:
time: 59.1 us; the launch traced here: 58.2 us
  Pallas kernels  44.6 us (75%)
  starting transfers between devices  12.8 us (22%)
  waiting for transfers between devices  0.68 us (1%)
    pallas_call x3, Pallas kernels, phase(): pl.pallas_call(functools.partial(phase_kernel, nb, tuple(chain), carry_in...  42.1 us
    ppermute x6, starting transfers between devices, from_partner(): lax.ppermute(x, axis, [(i, i ^ 1 << stride) for i in range(lax.axis_size(...  12.8 us
    pallas_call x1, Pallas kernels, start(): pl.pallas_call(functools.partial(start_kernel, nb, rounds), out_shape=[ja...  2.48 us
  transfers between devices with their start and end apart: 6, of which 1 were waited for; matrix products, arithmetic and copies ran while one was open for 0% of the time, Pallas kernels for 43%

profile of v3, /device:TPU:0, one launch (start us, length us, event | category | flops | bytes accessed | tf_op | source)
XLA Modules:
  0.0 58.2 jit_solution(8604812751847517728)
XLA Ops:
  0.0 2.5 %start.1 = (f32[1152,128]{1,0:T(8,128)S(1)}, s32[32,128]{1,0:T(8,128)S(1)}) custom-call(f32[3,24576]{1,0:T(4,128)} %refs_0_.1, f32[3,24576]{1,0:T(4,128)} %refs_1_.1, f32[192,128]{1,0:T(8,128)} %bitcast.8, s32[6,2,192]{2,1,0:T(2,128)} %bitcast.9, s32[6,192]{1,0:T(8,128)} %bitcast.10), custom_call_target="tpu_custom_call" | custom-call | tf_op jit(solution)/shard_map/start/pallas_call | solution.py:245
  2.5 0.1 collective-permute-start.5
  2.6 4.0 %collective-permute-start.2 = (f32[1152,128]{1,0:T(8,128)S(1)}, f32[1152,128]{1,0:T(8,128)S(1)}, u32[]{:S(2)}, u32[]{:S(2)}) collective-permute-start(f32[1152,128]{1,0:T(8,128)S(1)} %get-tuple-element.13.refs_0_), channel_id=1, source_target_pairs={{0,64},{4,68},{8,72},{12,76},{16,80},{20,84},{24,88},{28,92},{32,9... | collective-permute-start | bytes 1769480 | tf_op jit(solution)/shard_map/ppermute | solution.py:21
  6.6 1.5 %collective-permute-start.3 = (f32[1152,128]{1,0:T(8,128)S(1)}, f32[1152,128]{1,0:T(8,128)S(1)}, u32[]{:S(2)}, u32[]{:S(2)}) collective-permute-start(f32[1152,128]{1,0:T(8,128)S(1)} %get-tuple-element.13.refs_0_), channel_id=1, source_target_pairs={{0,2},{1,3},{2,0},{3,1},{4,6},{5,7},{6,4},{7,5},{8,10},{9,11},{10,... | collective-permute-start | bytes 1769480 | tf_op jit(solution)/shard_map/ppermute | solution.py:21
  8.1 1.6 %collective-permute-start.4 = (f32[1152,128]{1,0:T(8,128)S(1)}, f32[1152,128]{1,0:T(8,128)S(1)}, u32[]{:S(2)}, u32[]{:S(2)}) collective-permute-start(f32[1152,128]{1,0:T(8,128)S(1)} %get-tuple-element.13.refs_0_), channel_id=1, source_target_pairs={{0,4},{4,0},{8,12},{12,8},{16,20},{20,16},{24,28},{28,24},{32,36},... | collective-permute-start | bytes 1769480 | tf_op jit(solution)/shard_map/ppermute | solution.py:21
  9.7 2.9 %collective-permute-start = (f32[1152,128]{1,0:T(8,128)S(1)}, f32[1152,128]{1,0:T(8,128)S(1)}, u32[]{:S(2)}, u32[]{:S(2)}) collective-permute-start(f32[1152,128]{1,0:T(8,128)S(1)} %get-tuple-element.13.refs_0_), channel_id=1, source_target_pairs={{0,8},{4,12},{8,0},{12,4},{16,24},{20,28},{24,16},{28,20},{32,40},... | collective-permute-start | bytes 1769480 | tf_op jit(solution)/shard_map/ppermute | solution.py:21
  12.6 0.0 collective-permute-done.5.refs_1_
  12.6 2.7 %collective-permute-start.1 = (f32[1152,128]{1,0:T(8,128)S(1)}, f32[1152,128]{1,0:T(8,128)S(1)}, u32[]{:S(2)}, u32[]{:S(2)}) collective-permute-start(f32[1152,128]{1,0:T(8,128)S(1)} %get-tuple-element.13.refs_0_), channel_id=1, source_target_pairs={{0,16},{4,20},{8,24},{12,28},{16,0},{20,4},{24,8},{28,12},{32,48},... | collective-permute-start | bytes 1769480 | tf_op jit(solution)/shard_map/ppermute | solution.py:21
  15.3 8.3 %own_core.1 = (f32[192,8,128]{2,1,0:T(8,128)S(1)}, bf16[193,48,256]{2,1,0:T(8,128)(2,1)S(1)}, bf16[24576,128]{1,0:T(8,128)(2,1)S(1)}) custom-call(s32[4096]{0:T(1024)S(1)} %bitcast.5, f32[1152,128]{1,0:T(8,128)S(1)} %get-tuple-element.13.refs_0_, f32[1152,128]{1,0:T(8,128)S(1)} %collective-permute-done.5.refs_1_), custom_call_target="tpu_custom_call" | custom-call | flops 4000000000 | bytes 2000000 | tf_op jit(solution)/shard_map/own_core/pallas_call | solution.py:166
  23.6 0.0 collective-permute-done.2.refs_0_
  23.6 0.0 collective-permute-done.3.refs_1_
  23.7 0.7 %collective-permute-done.4.refs_2_ = f32[1152,128]{1,0:T(8,128)S(1)} collective-permute-done((f32[1152,128]{1,0:T(8,128)S(1)}, f32[1152,128]{1,0:T(8,128)S(1)}, u32[]{:S(2)}, u32[]{:S(2)}) %collective-permute-start.4) | collective-permute-done | bytes 589856 | tf_op jit(solution)/shard_map/ppermute | solution.py:21
  24.3 16.6 %mid.1 = (f32[192,8,128]{2,1,0:T(8,128)S(1)}, bf16[24576,128]{1,0:T(8,128)(2,1)S(1)}) custom-call(s32[4096]{0:T(1024)S(1)} %bitcast.6, f32[1152,128]{1,0:T(8,128)S(1)} %collective-permute-done.2.refs_0_, f32[1152,128]{1,0:T(8,128)S(1)} %collective-permute-done.3.refs_1_, f32[1152,128]{1,0:T(8,128)S(1)} %collective-permute-done.4.refs_2_, ...), custom_call_target="tpu_custom_call" | custom-call | flops 8000000000 | bytes 4000000 | tf_op jit(solution)/shard_map/mid/pallas_call | solution.py:166
  40.9 0.0 collective-permute-done.refs_0_
  40.9 0.0 collective-permute-done.1.refs_1_
  40.9 17.3 %end.1 = f32[192,128]{1,0:T(8,128)} custom-call(s32[4096]{0:T(1024)S(1)} %bitcast.7, f32[1152,128]{1,0:T(8,128)S(1)} %collective-permute-done.refs_0_, f32[1152,128]{1,0:T(8,128)S(1)} %collective-permute-done.1.refs_1_, f32[192,8,128]{2,1,0:T(8,128)S(1)} %get-tuple-element.17.refs_2_, bf16[193,48,256]{2,1,0:T(8,128)(2,1)S(1)} %get-tuple-element.15.refs_4_.refs_3_, ...), custom_call_target="tpu_custom_call" | custom-call | flops 6000000000 | bytes 3000000 | tf_op jit(solution)/shard_map/end/pallas_call | solution.py:166
Async XLA Ops:
  2.5 10.1 %collective-permute-start.5 = (f32[1152,128]{1,0:T(8,128)S(1)}, f32[1152,128]{1,0:T(8,128)S(1)}, u32[]{:S(2)}, u32[]{:S(2)}) collective-permute-start(f32[1152,128]{1,0:T(8,128)S(1)} %get-tuple-element.13.refs_0_), channel_id=1, source_target_pairs={{0,1},{1,0},{2,3},{3,2},{4,5},{5,4},{6,7},{7,6},{8,9},{9,8},{10,11... | collective-permute-start | bytes 1769480 | tf_op jit(solution)/shard_map/ppermute | solution.py:21
  2.6 21.1 %collective-permute-start.2 = (f32[1152,128]{1,0:T(8,128)S(1)}, f32[1152,128]{1,0:T(8,128)S(1)}, u32[]{:S(2)}, u32[]{:S(2)}) collective-permute-start(f32[1152,128]{1,0:T(8,128)S(1)} %get-tuple-element.13.refs_0_), channel_id=1, source_target_pairs={{0,64},{4,68},{8,72},{12,76},{16,80},{20,84},{24,88},{28,92},{32,9... | collective-permute-start | bytes 1769480 | tf_op jit(solution)/shard_map/ppermute | solution.py:21
  6.6 17.0 %collective-permute-start.3 = (f32[1152,128]{1,0:T(8,128)S(1)}, f32[1152,128]{1,0:T(8,128)S(1)}, u32[]{:S(2)}, u32[]{:S(2)}) collective-permute-start(f32[1152,128]{1,0:T(8,128)S(1)} %get-tuple-element.13.refs_0_), channel_id=1, source_target_pairs={{0,2},{1,3},{2,0},{3,1},{4,6},{5,7},{6,4},{7,5},{8,10},{9,11},{10,... | collective-permute-start | bytes 1769480 | tf_op jit(solution)/shard_map/ppermute | solution.py:21
  8.1 16.2 %collective-permute-start.4 = (f32[1152,128]{1,0:T(8,128)S(1)}, f32[1152,128]{1,0:T(8,128)S(1)}, u32[]{:S(2)}, u32[]{:S(2)}) collective-permute-start(f32[1152,128]{1,0:T(8,128)S(1)} %get-tuple-element.13.refs_0_), channel_id=1, source_target_pairs={{0,4},{4,0},{8,12},{12,8},{16,20},{20,16},{24,28},{28,24},{32,36},... | collective-permute-start | bytes 1769480 | tf_op jit(solution)/shard_map/ppermute | solution.py:21
  9.7 31.2 %collective-permute-start = (f32[1152,128]{1,0:T(8,128)S(1)}, f32[1152,128]{1,0:T(8,128)S(1)}, u32[]{:S(2)}, u32[]{:S(2)}) collective-permute-start(f32[1152,128]{1,0:T(8,128)S(1)} %get-tuple-element.13.refs_0_), channel_id=1, source_target_pairs={{0,8},{4,12},{8,0},{12,4},{16,24},{20,28},{24,16},{28,20},{32,40},... | collective-permute-start | bytes 1769480 | tf_op jit(solution)/shard_map/ppermute | solution.py:21
  12.6 28.3 %collective-permute-start.1 = (f32[1152,128]{1,0:T(8,128)S(1)}, f32[1152,128]{1,0:T(8,128)S(1)}, u32[]{:S(2)}, u32[]{:S(2)}) collective-permute-start(f32[1152,128]{1,0:T(8,128)S(1)} %get-tuple-element.13.refs_0_), channel_id=1, source_target_pairs={{0,16},{4,20},{8,24},{12,28},{16,0},{20,4},{24,8},{28,12},{32,48},... | collective-permute-start | bytes 1769480 | tf_op jit(solution)/shard_map/ppermute | solution.py:21
